TPU v7x, 32 devices: a whole 2x2x4 slice. The times are simulated.
32 devices in a mesh: dp: 4 (over z), shard: 8 (over y, x, core).
Axes of the slice: x: 2, y: 2, z: 4, core: 2. Of those that a mesh axis runs over, the one named last changes fastest.
Arguments:
- grad: bfloat16 [4, 4, 2, 1024, 8192], P('dp', None, None, 'shard'), may hold values from -6 to 6
- error: bfloat16 [4, 4, 2, 1024, 8192], P('dp', None, None, 'shard'), may hold values from -4 to 4
- q_prev: float32 [4, 2, 8, 8192], replicated, may hold values from -6 to 6
Outputs:
- error_out: bfloat16 [4, 4, 2, 1024, 8192], P('dp', None, None, 'shard')
- approx: float32 [4, 2, 1024, 8192], P(None, None, 'shard')
- q_new: float32 [4, 2, 8, 8192], replicated
All inputs are finite; a program needn't handle non-finite values.
Results may differ from a plain program's by a relative error of at most 0.0014.
Values sent between devices are 32-bit elements; how exact they have to be, the bound alone decides.
No kernel may reach another device: no remote copies, remote signals or barrier semaphores. Data moves between devices by JAX's collectives and lax.ppermute only.
A program may use at most 192 MiB of HBM per device.

v0:
```python
import jax
import jax.numpy as jnp
from jax import lax
from jax.sharding import PartitionSpec as P


def on_device(grad, error, q_prev):
    highest = lax.Precision.HIGHEST
    groups, layers, pair, rows, width = grad.shape
    matrices = layers * pair
    rank = q_prev.shape[2]
    merged = (grad.astype(jnp.float32) + error.astype(jnp.float32)).reshape(matrices, rows, width)
    basis = q_prev.reshape(matrices, rank, width)
    part = jnp.einsum("mrd,mkd->mrk", merged, basis, precision=highest)
    summed = lax.psum(part, "dp")
    p_orth = jnp.zeros_like(summed)
    column_ids = jnp.arange(rank)
    for index in range(rank):
        column = summed[:, :, index]
        coef = lax.psum(jnp.einsum("mrk,mr->mk", p_orth, column, precision=highest), "shard")
        column = column - jnp.einsum("mrk,mk->mr", p_orth, coef, precision=highest)
        norm = lax.psum(jnp.sum(column * column, axis=1), "shard")
        column = column / jnp.sqrt(norm)[:, None]
        p_orth = jnp.where((column_ids == index)[None, None, :], column[:, :, None], p_orth)
    local_q = jnp.einsum("mrd,mrk->mkd", merged, p_orth, precision=highest)
    total_q = lax.psum(local_q, ("dp", "shard"))
    q_new = total_q / lax.axis_size("dp")
    approx = jnp.einsum("mrk,mkd->mrd", p_orth, q_new, precision=highest)
    error_out = (merged - approx).astype(jnp.bfloat16).reshape(grad.shape)
    return (error_out, approx.reshape(layers, pair, rows, width), q_new.reshape(q_prev.shape))


def solution(mesh):
    in_specs = (P("dp", None, None, "shard", None), P("dp", None, None, "shard", None), P())
    out_specs = (P("dp", None, None, "shard", None), P(None, None, "shard", None), P())
    return jax.shard_map(
        on_device, mesh=mesh, in_specs=in_specs, out_specs=out_specs, check_vma=False
    )
```

profile of v0, /device:TPU:0, one launch (start us, length us, event | category | flops | bytes accessed | tf_op | source)
XLA Modules:
  0.0 476.2 jit_solution(2387440960428433905)
XLA Ops:
  7.3 23.5 %convert_add_fusion = f32[1,4,2,128,8192]{4,3,2,1,0:T(8,128)} fusion(bf16[1,4,2,128,8192]{4,3,2,1,0:T(8,128)(2,1)} %param.4, bf16[1,4,2,128,8192]{4,3,2,1,0:T(8,128)(2,1)} %param.3), kind=kLoop, calls=%fused_computation.1 | loop fusion | flops 25165824 | bytes 67108864 | tf_op jit(solution)/shard_map/add | solution.py:12
  30.8 31.7 %fusion.226 = f32[8,128,8]{1,2,0:T(8,128)S(1)} fusion(f32[8,128,8192]{2,1,0:T(8,128)} %bitcast.107, f32[8,8,8192]{2,1,0:T(8,128)S(1)} %bitcast.106), kind=kOutput, calls=%fused_computation.242 | convolution fusion | flops 805306368 | bytes 35684352 | tf_op jit(solution)/shard_map/mrd,mkd->mrk/dot_general | solution.py:14
  62.5 20.8 %psum.126 = f32[8,128,8]{1,2,0:T(8,128)S(1)} all-reduce(f32[8,128,8]{1,2,0:T(8,128)S(1)} %fusion.226), channel_id=1, replica_groups=mesh['dp'=4,'shard'=8] {'dp'}, use_global_device_ids=true, to_apply=%region_0.0 | all-reduce | flops 8192 | bytes 65536 | tf_op jit(solution)/shard_map/psum | solution.py:15
  83.5 11.8 %psum.127 = f32[8,8]{1,0:T(8,128)S(1)} all-reduce(f32[8,8]{1,0:T(8,128)S(1)} %bitcast.137), channel_id=1, replica_groups=mesh['dp'=4,'shard'=8] {'shard'}, use_global_device_ids=true, to_apply=%region_1.0 | all-reduce | flops 64 | bytes 512 | tf_op jit(solution)/shard_map/psum | solution.py:20
  95.7 11.9 %psum.128 = f32[8]{0:T(128)S(1)} all-reduce(f32[8]{0:T(128)S(1)} %get-tuple-element.17), channel_id=1, replica_groups=mesh['dp'=4,'shard'=8] {'shard'}, use_global_device_ids=true, to_apply=%region_3.0 | all-reduce | flops 8 | bytes 64 | tf_op jit(solution)/shard_map/psum | solution.py:22
  107.7 0.3 fusion.2
  108.0 11.8 %psum.129 = f32[8,8]{1,0:T(8,128)S(1)} all-reduce(f32[8,8]{1,0:T(8,128)S(1)} %bitcast.138), channel_id=1, replica_groups=mesh['dp'=4,'shard'=8] {'shard'}, use_global_device_ids=true, to_apply=%region_4.5 | all-reduce | flops 64 | bytes 512 | tf_op jit(solution)/shard_map/psum | solution.py:20
  120.1 11.8 %psum.130 = f32[8]{0:T(128)S(1)} all-reduce(f32[8]{0:T(128)S(1)} %get-tuple-element.15), channel_id=1, replica_groups=mesh['dp'=4,'shard'=8] {'shard'}, use_global_device_ids=true, to_apply=%region_6.7 | all-reduce | flops 8 | bytes 64 | tf_op jit(solution)/shard_map/psum | solution.py:22
  132.0 0.3 fusion.6
  132.3 11.8 %psum.131 = f32[8,8]{1,0:T(8,128)S(1)} all-reduce(f32[8,8]{1,0:T(8,128)S(1)} %bitcast.139), channel_id=1, replica_groups=mesh['dp'=4,'shard'=8] {'shard'}, use_global_device_ids=true, to_apply=%region_7.8 | all-reduce | flops 64 | bytes 512 | tf_op jit(solution)/shard_map/psum | solution.py:20
  144.5 11.8 %psum.132 = f32[8]{0:T(128)S(1)} all-reduce(f32[8]{0:T(128)S(1)} %get-tuple-element.13), channel_id=1, replica_groups=mesh['dp'=4,'shard'=8] {'shard'}, use_global_device_ids=true, to_apply=%region_9.10 | all-reduce | flops 8 | bytes 64 | tf_op jit(solution)/shard_map/psum | solution.py:22
  156.4 0.3 fusion.10
  156.6 11.8 %psum.133 = f32[8,8]{1,0:T(8,128)S(1)} all-reduce(f32[8,8]{1,0:T(8,128)S(1)} %bitcast.140), channel_id=1, replica_groups=mesh['dp'=4,'shard'=8] {'shard'}, use_global_device_ids=true, to_apply=%region_10.11 | all-reduce | flops 64 | bytes 512 | tf_op jit(solution)/shard_map/psum | solution.py:20
  168.8 11.8 %psum.134 = f32[8]{0:T(128)S(1)} all-reduce(f32[8]{0:T(128)S(1)} %get-tuple-element.11), channel_id=1, replica_groups=mesh['dp'=4,'shard'=8] {'shard'}, use_global_device_ids=true, to_apply=%region_12.13 | all-reduce | flops 8 | bytes 64 | tf_op jit(solution)/shard_map/psum | solution.py:22
  180.7 0.3 fusion.15
  181.0 11.8 %psum.135 = f32[8,8]{1,0:T(8,128)S(1)} all-reduce(f32[8,8]{1,0:T(8,128)S(1)} %bitcast.141), channel_id=1, replica_groups=mesh['dp'=4,'shard'=8] {'shard'}, use_global_device_ids=true, to_apply=%region_13.14 | all-reduce | flops 64 | bytes 512 | tf_op jit(solution)/shard_map/psum | solution.py:20
  193.2 11.8 %psum.136 = f32[8]{0:T(128)S(1)} all-reduce(f32[8]{0:T(128)S(1)} %get-tuple-element.9), channel_id=1, replica_groups=mesh['dp'=4,'shard'=8] {'shard'}, use_global_device_ids=true, to_apply=%region_15.16 | all-reduce | flops 8 | bytes 64 | tf_op jit(solution)/shard_map/psum | solution.py:22
  205.0 0.3 fusion.20
  205.3 11.8 %psum.137 = f32[8,8]{1,0:T(8,128)S(1)} all-reduce(f32[8,8]{1,0:T(8,128)S(1)} %bitcast.142), channel_id=1, replica_groups=mesh['dp'=4,'shard'=8] {'shard'}, use_global_device_ids=true, to_apply=%region_16.17 | all-reduce | flops 64 | bytes 512 | tf_op jit(solution)/shard_map/psum | solution.py:20
  217.1 0.3 fusion.18
  217.5 11.8 %psum.138 = f32[8]{0:T(128)S(1)} all-reduce(f32[8]{0:T(128)S(1)} %get-tuple-element.7), channel_id=1, replica_groups=mesh['dp'=4,'shard'=8] {'shard'}, use_global_device_ids=true, to_apply=%region_18.19 | all-reduce | flops 8 | bytes 64 | tf_op jit(solution)/shard_map/psum | solution.py:22
  229.4 0.3 fusion.25
  229.7 11.8 %psum.139 = f32[8,8]{1,0:T(8,128)S(1)} all-reduce(f32[8,8]{1,0:T(8,128)S(1)} %bitcast.143), channel_id=1, replica_groups=mesh['dp'=4,'shard'=8] {'shard'}, use_global_device_ids=true, to_apply=%region_19.20 | all-reduce | flops 64 | bytes 512 | tf_op jit(solution)/shard_map/psum | solution.py:20
  241.5 0.3 fusion.23
  241.9 11.8 %psum.140 = f32[8]{0:T(128)S(1)} all-reduce(f32[8]{0:T(128)S(1)} %get-tuple-element.5), channel_id=1, replica_groups=mesh['dp'=4,'shard'=8] {'shard'}, use_global_device_ids=true, to_apply=%region_21.22 | all-reduce | flops 8 | bytes 64 | tf_op jit(solution)/shard_map/psum | solution.py:22
  253.7 0.3 fusion.30
  254.0 11.8 %psum.141 = f32[8,8]{1,0:T(8,128)S(1)} all-reduce(f32[8,8]{1,0:T(8,128)S(1)} %bitcast.135), channel_id=1, replica_groups=mesh['dp'=4,'shard'=8] {'shard'}, use_global_device_ids=true, to_apply=%region_22.23 | all-reduce | flops 64 | bytes 512 | tf_op jit(solution)/shard_map/psum | solution.py:20
  266.2 12.0 %psum.142 = f32[8]{0:T(128)S(1)} all-reduce(f32[8]{0:T(128)S(1)} %get-tuple-element.3), channel_id=1, replica_groups=mesh['dp'=4,'shard'=8] {'shard'}, use_global_device_ids=true, to_apply=%region_24.25 | all-reduce | flops 8 | bytes 64 | tf_op jit(solution)/shard_map/psum | solution.py:22
  278.3 20.3 %fusion.34 = f32[8,8,8192]{2,1,0:T(8,128)} fusion(f32[8,128,8192]{2,1,0:T(8,128)} %bitcast.108, f32[8,128]{1,0:T(8,128)S(1)} %broadcast_divide_fusion, f32[8,128]{1,0:T(8,128)S(1)} %broadcast_divide_fusion.1, f32[8,128]{1,0:T(8,128)S(1)} %broadcast_divide_fusion.2, f32[8,128]{1,0:T(8,128)S(1)} %broadcast_divide_fusion.3, ...), kind=kOutput, calls=%fused_computation.27 | convolution fusion | flops 805371904 | bytes 35684416 | tf_op jit(solution)/shard_map/mrd,mrk->mkd/dot_general | solution.py:25
  298.6 131.3 %all-reduce.2.cloned.1.call-done = f32[8,8,8192]{2,1,0:T(8,128)} async-done(((f32[8,8,8192]{2,1,0:T(8,128)}), f32[8,8,8192]{2,1,0:T(8,128)}) %all-reduce.2.cloned.1.call-update) | async-done | bytes 2097168 | tf_op jit(solution)/shard_map/psum | solution.py:26
  429.9 37.9 %subtract_convert_fusion = (bf16[8,128,8192]{2,1,0:T(8,128)(2,1)}, f32[8,128,8192]{2,1,0:T(8,128)}) fusion(f32[1,4,2,128,8192]{4,3,2,1,0:T(8,128)} %convert_add_fusion, f32[8,8,8192]{2,1,0:T(8,128)} %all-reduce.2.cloned.1.call-done, f32[8,128]{1,0:T(8,128)S(1)} %broadcast_divide_fusion, f32[8,128]{1,0:T(8,128)S(1)} %broadcast_divide_fusion.1, ...), kind=kOutput, calls=%fused_computation | convolution fusion | flops 822673408 | bytes 86016064 | tf_op jit(solution)/shard_map/mrk,mkd->mrd/dot_general | solution.py:28
  467.8 1.5 broadcast_multiply_fusion
  (48 shorter events, 3.4 us)
Async XLA Ops:
  7.2 23.7 %copy-start = (f32[4,2,8,8192]{3,2,1,0:T(8,128)S(1)}, f32[4,2,8,8192]{3,2,1,0:T(8,128)}, u32[]{:S(2)}) copy-start(f32[4,2,8,8192]{3,2,1,0:T(8,128)} %param.5) | copy-start | bytes 6291460
  7.2 422.7 %all-reduce.2.cloned.1.call-start = ((), (), s32[]{:S(2)}) async-start(), calls=%async_computation | async-start | bytes 4194304 | tf_op jit(solution)/shard_map/psum | solution.py:26
  429.9 37.9 %copy-start.2 = (f32[8,8,8192]{2,1,0:T(8,128)S(1)}, f32[8,8,8192]{2,1,0:T(8,128)}, u32[]{:S(2)}) copy-start(f32[8,8,8192]{2,1,0:T(8,128)} %all-reduce.2.cloned.1.call-done) | copy-start | bytes 6291460
  429.9 39.4 %copy-start.1 = (f32[4,2,8,8192]{3,2,1,0:T(8,128)S(1)}, f32[4,2,8,8192]{3,2,1,0:T(8,128)}, u32[]{:S(2)}) copy-start(f32[4,2,8,8192]{3,2,1,0:T(8,128)} %param.5) | copy-start | bytes 6291460
Sparse Core Ops, SparseCore 0:
  298.7 131.0 all-reduce.1
where the time goes:
time: 477 us; the launch traced here: 476 us
  blocking collectives  210 us (44%)
  waiting for transfers between devices  131 us (27%)
  matrix products  94.1 us (20%)
  other arithmetic  26.6 us (6%)
  between operations  14.2 us (3%)
    psum x1, waiting for transfers between devices, on_device(): total_q = lax.psum(local_q, ('dp', 'shard'))  131 us
    psum x8, blocking collectives, on_device(): norm = lax.psum(jnp.sum(column * column, axis=1), 'shard')  94.6 us
    psum x8, blocking collectives, on_device(): lax.psum(jnp.einsum('mrk,mr->mk', p_orth, column, precision=highest), 'sh...  94.5 us
    dot_general x1, matrix products, on_device(): approx = jnp.einsum('mrk,mkd->mrd', p_orth, q_new, precision=highest)  37.9 us
    dot_general x1, matrix products, on_device(): part = jnp.einsum('mrd,mkd->mrk', merged, basis, precision=highest)  31.7 us
    add x1, other arithmetic, on_device(): grad.astype(jnp.float32) + error.astype(jnp.float32)  23.5 us
    psum x1, blocking collectives, on_device(): summed = lax.psum(part, 'dp')  20.8 us
    dot_general x1, matrix products, on_device(): local_q = jnp.einsum('mrd,mrk->mkd', merged, p_orth, precision=highest)  20.3 us
  transfers between devices with their start and end apart: 1, of which 1 were waited for; matrix products, arithmetic and copies ran while one was open for 0% of the time, Pallas kernels for 0%

commit v1 on v0

v1 whole, which is shorter than its diff:
```python
import functools

import jax
import jax.numpy as jnp
from jax import lax
from jax.experimental import pallas as pl
from jax.experimental.pallas import tpu as pltpu
from jax.sharding import PartitionSpec as P

F32 = jnp.float32
BF16 = jnp.bfloat16
LANES = 128
MIB = 1 << 20


def split3(x):
    hi = x.astype(BF16).astype(F32)
    rest = x - hi
    mid = rest.astype(BF16).astype(F32)
    low = (rest - mid).astype(BF16).astype(F32)
    return hi, mid, low


def tree_sum(terms):
    terms = list(terms)
    while len(terms) > 1:
        terms = [terms[i] + terms[i + 1] for i in range(0, len(terms), 2)]
    return terms[0]


def left_kernel(g_hbm, e_hbm, q_hbm, g_out, e_out, p_out, q_in, sems, q_sem):
    matrices, rows, _ = g_out.shape
    rank = q_in.shape[1]

    def pair(m):
        return (
            pltpu.make_async_copy(g_hbm.at[m], g_out.at[m], sems.at[0, m]),
            pltpu.make_async_copy(e_hbm.at[m], e_out.at[m], sems.at[1, m]),
        )

    q_copy = pltpu.make_async_copy(q_hbm, q_in, q_sem)
    q_copy.start()
    for m in range(matrices):
        for copy in pair(m):
            copy.start()
    q_copy.wait()

    @pl.loop(0, matrices)
    def _(m):
        basis = jnp.concatenate(split3(q_in[m]), axis=0).astype(BF16)
        for copy in pair(m):
            copy.wait()
        both = jnp.concatenate([g_out[m], e_out[m]], axis=0)
        part = lax.dot_general(both, basis, (((1,), (1,)), ((), ())), preferred_element_type=F32)
        part = (part[:rows] + part[rows:]).T
        p_out[m] = part[:rank] + (part[rank : 2 * rank] + part[2 * rank :])


def right_kernel(me_ref, g_ref, e_ref, *refs, pieces, blocks):
    p_refs, (sum_out, gram_out, *outs), (left,) = refs[: -3 - blocks], refs[-3 - blocks : -1], refs[-1:]
    matrices, rows, width = g_ref.shape
    rank = sum_out.shape[1]
    p_sum = tree_sum([r[...] for r in p_refs])
    sum_out[...] = p_sum
    lane = lax.broadcasted_iota(jnp.int32, (rank, LANES), 1)
    gram = jnp.zeros((rank, LANES), F32)
    for m in range(matrices):
        one = p_sum[m]
        for j in range(rank):
            column = jnp.sum(one * one[j : j + 1], axis=1, keepdims=True)
            gram = jnp.where(lane == j * matrices + m, column, gram)
        terms = jnp.concatenate(split3(one), axis=0)
        left[m] = jnp.concatenate([terms, terms], axis=1).astype(BF16)
    gram_out[...] = gram
    me = me_ref[0]
    per = pieces // matrices
    columns = width // per
    each = pieces // blocks

    for block in range(blocks):

        @pl.loop(0, each)
        def _(slot):
            piece = jnp.bitwise_xor(slot + block * each, me)
            m = piece // per
            start = pl.multiple_of(lax.rem(piece, per) * columns, columns)
            both = jnp.concatenate(
                [g_ref[m, :, pl.ds(start, columns)], e_ref[m, :, pl.ds(start, columns)]], axis=0
            )
            part = jnp.dot(left[m], both, preferred_element_type=F32)
            part = part[:rank] + (part[rank : 2 * rank] + part[2 * rank :])
            for t in range(columns // LANES):
                outs[block][slot, t] = part[:, t * LANES : (t + 1) * LANES]


def invert(gram, matrices, rank):
    row = lax.broadcasted_iota(jnp.int32, (rank, LANES), 0)
    lane = lax.broadcasted_iota(jnp.int32, (rank, LANES), 1)
    used = lane < matrices
    unit = [jnp.where(row == j, 1.0, 0.0).astype(F32) for j in range(rank)]
    cols = [
        jnp.where(used, gram if j == 0 else pltpu.roll(gram, LANES - j * matrices, 1), unit[j]) for j in range(rank)
    ]
    inverse = list(unit)
    scale = jnp.ones((rank, LANES), F32)
    for k in range(rank):
        pivot = jnp.broadcast_to(cols[k][k : k + 1], (rank, LANES))
        scale = jnp.where(row == k, 1.0 / jnp.sqrt(pivot), scale)
        factor = jnp.where(row > k, cols[k] / pivot, 0.0)
        for j in range(k + 1, rank):
            cols[j] = cols[j] - factor * cols[j][k : k + 1]
        for j in range(k + 1):
            inverse[j] = inverse[j] - factor * inverse[j][k : k + 1]
    return [scale * c for c in inverse]


def piece_kernel(me_ref, gram_ref, *refs, pieces, matrices, groups):
    part_refs, (q_out, inv_out) = refs[:-2], refs[-2:]
    rank = gram_ref.shape[0]
    inverse = invert(gram_ref[...], matrices, rank)
    for j in range(rank):
        inv_out[j] = inverse[j]
    m = me_ref[0] // (pieces // matrices)
    lane = lax.broadcasted_iota(jnp.int32, (rank, LANES), 1)
    picked = [
        jnp.broadcast_to(jnp.sum(jnp.where(lane == m, c, 0.0), axis=1, keepdims=True), (rank, LANES)) / groups
        for c in inverse
    ]
    for t in range(q_out.shape[0]):
        total = tree_sum([r[t] for r in part_refs])
        q_out[t] = sum(picked[j] * total[j : j + 1] for j in range(rank))


def out_kernel(me_ref, g_ref, e_ref, sum_ref, inv_ref, *refs, pieces, splits):
    q_refs, (err_out, approx_out, q_out, p_left) = refs[:-4], refs[-4:]
    m = pl.program_id(0)
    part = pl.program_id(1)
    matrices, rows, width = g_ref.shape
    rank = sum_ref.shape[1]
    per = pieces // matrices
    columns = width // per
    each = pieces // len(q_refs)

    @pl.when((m == 0) & (part == 0))
    def _():
        for block, ref in enumerate(q_refs):

            @pl.loop(0, each)
            def _(slot):
                piece = jnp.bitwise_xor(slot + block * each, me_ref[0])
                start = pl.multiple_of(lax.rem(piece, per) * columns, columns)
                for t in range(columns // LANES):
                    q_out[piece // per, :, pl.ds(start + t * LANES, LANES)] = ref[slot, t]

    @pl.when(part == 0)
    def _():
        lane = lax.broadcasted_iota(jnp.int32, (rank, LANES), 1)
        one = sum_ref[m]
        orth = jnp.zeros((rank, rows), F32)
        for j in range(rank):
            weight = jnp.sum(jnp.where(lane == m, inv_ref[j], 0.0), axis=1, keepdims=True)
            orth = orth + weight * one[j : j + 1]
        hi = orth.astype(BF16).astype(F32)
        low = (orth - hi).astype(BF16).astype(F32)
        p_left[...] = jnp.concatenate([hi, low, hi], axis=0).T.astype(BF16)

    step = min(columns, width // splits)
    for k in range(width // splits // step):
        start = pl.multiple_of(part * (width // splits) + k * step, step)
        right = q_out[m, :, pl.ds(start, step)]
        hi = right.astype(BF16).astype(F32)
        low = (right - hi).astype(BF16).astype(F32)
        terms = jnp.concatenate([hi, hi, low], axis=0).astype(BF16)
        approx = jnp.dot(p_left[...], terms, preferred_element_type=F32)
        here = pl.ds(k * step, step)
        approx_out[0, :, here] = approx
        merged = g_ref[m, :, pl.ds(start, step)].astype(F32) + e_ref[m, :, pl.ds(start, step)].astype(F32)
        err_out[0, :, here] = (merged - approx).astype(BF16)


def on_device(sizes, grad, error, q_prev):
    groups, shards = sizes
    _, layers, pair, rows, width = grad.shape
    matrices = layers * pair
    rank = q_prev.shape[2]
    pieces = groups * shards
    chips = shards // 2
    stages = [("shard", 1, 2)]
    step = 2
    while chips > 1:
        count = min(4, chips)
        stages.append(("shard", step, count))
        step, chips = step * count, chips // count
    stages.append(("dp", 1, groups))
    me = jnp.int32(0)
    for name, step, count in stages:
        me = me * count + (lax.axis_index(name) // step) % count
    me = me.reshape(1)
    tiles = matrices * width // pieces // LANES

    vmem = pl.BlockSpec(memory_space=pltpu.VMEM)
    smem = pl.BlockSpec(memory_space=pltpu.SMEM)
    anywhere = pl.BlockSpec(memory_space=pl.ANY)

    def swap(x, name, step, k):
        size = sizes[0] if name == "dp" else sizes[1]
        return lax.ppermute(x, name, [(i, i ^ (k * step)) for i in range(size)])

    def pinned(x):
        return pltpu.with_memory_space_constraint(x, pltpu.VMEM)

    block = (matrices, rows, width)
    g_keep, e_keep, p_own = pl.pallas_call(
        left_kernel,
        out_shape=(
            pltpu.VMEM(block, BF16),
            pltpu.VMEM(block, BF16),
            jax.ShapeDtypeStruct((matrices, rank, rows), F32),
        ),
        in_specs=[anywhere] * 3,
        out_specs=(vmem, vmem, vmem),
        scratch_shapes=[
            pltpu.VMEM((matrices, rank, width), F32),
            pltpu.SemaphoreType.DMA((2, matrices)),
            pltpu.SemaphoreType.DMA,
        ],
        compiler_params=pltpu.CompilerParams(vmem_limit_bytes=8 * MIB),
        name="left",
    )(grad.reshape(block), error.reshape(block), q_prev.reshape(matrices, rank, width))

    p_all = [p_own] + [swap(p_own, "dp", 1, k) for k in range(1, groups)]

    each = pieces // 2
    p_sum, gram, *halves = pl.pallas_call(
        functools.partial(right_kernel, pieces=pieces, blocks=2),
        out_shape=(
            jax.ShapeDtypeStruct((matrices, rank, rows), F32),
            jax.ShapeDtypeStruct((rank, LANES), F32),
        )
        + (jax.ShapeDtypeStruct((each, tiles, rank, LANES), F32),) * 2,
        in_specs=[smem] + [vmem] * (2 + groups),
        out_specs=(vmem,) * 4,
        scratch_shapes=[pltpu.VMEM((matrices, 3 * rank, 2 * rows), BF16)],
        compiler_params=pltpu.CompilerParams(vmem_limit_bytes=10 * MIB),
        name="right",
    )(me, pinned(g_keep), pinned(e_keep), *p_all)

    for at, (name, step, count) in enumerate(stages):
        arrived = [swap(halves[k], name, step, k) for k in range(1, count)]
        if name == "shard":
            gram = tree_sum([gram] + [swap(gram, name, step, k) for k in range(1, count)])
        if at < len(stages) - 1:
            following = stages[at + 1][2]
            each //= following
            shape = (following, each, tiles, rank, LANES)
            terms = [x.reshape(shape) for x in [halves[0]] + arrived]
            halves = [tree_sum([x[k] for x in terms]) for k in range(following)]
    parts = [x.reshape(tiles, rank, LANES) for x in [halves[0]] + arrived]

    piece, inverse = pl.pallas_call(
        functools.partial(piece_kernel, pieces=pieces, matrices=matrices, groups=groups),
        out_shape=(
            jax.ShapeDtypeStruct((tiles, rank, LANES), F32),
            jax.ShapeDtypeStruct((rank, rank, LANES), F32),
        ),
        in_specs=[smem] + [vmem] * (1 + groups),
        out_specs=(vmem, vmem),
        compiler_params=pltpu.CompilerParams(vmem_limit_bytes=4 * MIB),
        name="piece",
    )(me, gram, *parts)

    ready = [piece.reshape(1, tiles, rank, LANES)]
    for name, step, count in reversed(stages):
        ready = ready + [swap(x, name, step, k) for k in range(1, count) for x in ready]
        if name == "dp":
            ready = [jnp.concatenate(ready, axis=0)]

    splits = 2
    out_block = (1, rows, width // splits)

    def whole_spec(space):
        return pl.BlockSpec(memory_space=space)

    error_out, approx, q_new = pl.pallas_call(
        functools.partial(out_kernel, pieces=pieces, splits=splits),
        grid=(matrices, splits),
        out_shape=(
            jax.ShapeDtypeStruct(block, BF16),
            jax.ShapeDtypeStruct(block, F32),
            jax.ShapeDtypeStruct((matrices, rank, width), F32),
        ),
        in_specs=[smem] + [vmem] * (4 + len(ready)),
        out_specs=(
            pl.BlockSpec(out_block, lambda m, s: (m, 0, s)),
            pl.BlockSpec(out_block, lambda m, s: (m, 0, s)),
            vmem,
        ),
        scratch_shapes=[pltpu.VMEM((rows, 3 * rank), BF16)],
        compiler_params=pltpu.CompilerParams(
            vmem_limit_bytes=16 * MIB, dimension_semantics=("arbitrary", "arbitrary")
        ),
        name="out",
    )(me, pinned(g_keep), pinned(e_keep), p_sum, inverse, *ready)
    return error_out.reshape(grad.shape), approx.reshape(layers, pair, rows, width), q_new.reshape(q_prev.shape)


def solution(mesh):
    sizes = (mesh.shape["dp"], mesh.shape["shard"])
    in_specs = (P("dp", None, None, "shard", None), P("dp", None, None, "shard", None), P())
    out_specs = (P("dp", None, None, "shard", None), P(None, None, "shard", None), P())
    return jax.shard_map(
        functools.partial(on_device, sizes), mesh=mesh, in_specs=in_specs, out_specs=out_specs, check_vma=False
    )
```

time: 477 us -> 143 us (0.30)
  blocking collectives: 210 us -> 0 us
  waiting for transfers between devices: 131 us -> 34.9 us
  matrix products: 94.1 us -> 0 us
  Pallas kernels: 0 us -> 43.4 us
  local copies, waits for them, and re-layouts: 0.11 us -> 37 us
  starting transfers between devices: 0.04 us -> 26.6 us
  other arithmetic: 26.6 us -> 0.22 us
  between operations: 14.2 us -> 0.72 us
    psum x17 -> x0, blocking collectives: 210 us -> none  [the longest x8 94.6 us: on_device(): norm = lax.psum(jnp.sum(column * column, axis=1), 'shard')]
    psum x1 -> x0, waiting for transfers between devices: 131 us -> none  [on_device(): total_q = lax.psum(local_q, ('dp', 'shard'))]
    dot_general x19 -> x0, matrix products: 94.1 us -> none  [the longest x1 37.9 us: on_device(): approx = jnp.einsum('mrk,mkd->mrd', p_orth, q_new, precision=highest)]
    pallas_call x0 -> x4, Pallas kernels: none -> 43.4 us  [the longest x1 20.3 us: on_device(): pl.pallas_call(functools.partial(out_kernel, pieces=pieces, splits=splits...]
    unnamed x6 -> x14, local copies, waits for them, and re-layouts: 0.02 us -> 37 us
    ppermute x0 -> x24, waiting for transfers between devices: none -> 34.9 us  [swap(): return lax.ppermute(x, name, [(i, i ^ k * step) for i in range(size)])]
    ppermute x0 -> x24, starting transfers between devices: none -> 26.6 us  [swap(): return lax.ppermute(x, name, [(i, i ^ k * step) for i in range(size)])]
    add x1 -> x4, other arithmetic: 23.5 us -> 0.2 us  [tree_sum(): terms = [terms[i] + terms[i + 1] for i in range(0, len(terms), 2)]]
  transfers between devices with their start and end apart: 1 -> 24, of which waited for: 1 -> 16; matrix products, arithmetic and copies ran while one was open for 0% -> 0% of each run, Pallas kernels for 0% -> 0%
where the time goes in v1:
time: 143 us
  Pallas kernels  43.4 us (30%)
  local copies, waits for them, and re-layouts  37 us (26%)
  waiting for transfers between devices  34.9 us (24%)
  starting transfers between devices  26.6 us (19%)
    unnamed x14, local copies, waits for them, and re-layouts  37 us
    ppermute x24, waiting for transfers between devices, swap(): return lax.ppermute(x, name, [(i, i ^ k * step) for i in range(size)])  34.9 us
    ppermute x24, starting transfers between devices, swap(): return lax.ppermute(x, name, [(i, i ^ k * step) for i in range(size)])  26.6 us
    pallas_call x1, Pallas kernels, on_device(): pl.pallas_call(functools.partial(out_kernel, pieces=pieces, splits=splits...  20.3 us
    pallas_call x1, Pallas kernels, on_device(): pl.pallas_call(left_kernel, out_shape=(pltpu.VMEM(block, BF16), pltpu.VME...  13.3 us
    pallas_call x1, Pallas kernels, on_device(): pl.pallas_call(functools.partial(right_kernel, pieces=pieces, blocks=2),...  9.49 us
  transfers between devices with their start and end apart: 24, of which 16 were waited for; matrix products, arithmetic and copies ran while one was open for 0% of the time, Pallas kernels for 0%

profile of v1, /device:TPU:0, one launch (start us, length us, event | category | flops | bytes accessed | tf_op | source)
XLA Modules:
  0.0 142.8 jit_solution(15473097087719944359)
XLA Ops:
  0.6 1.6 %copy-done.6 = f32[4,2,8,8192]{3,2,1,0:T(8,128)S(1)} copy-done((f32[4,2,8,8192]{3,2,1,0:T(8,128)S(1)}, f32[4,2,8,8192]{3,2,1,0:T(8,128)}, u32[]{:S(2)}) %copy-start.6) | copy-done | bytes 2097176
  2.2 13.3 %left.1 = (bf16[8,128,8192]{2,1,0:T(8,128)(2,1)S(1)}, bf16[8,128,8192]{2,1,0:T(8,128)(2,1)S(1)}, f32[8,8,128]{2,1,0:T(8,128)S(1)}) custom-call(bf16[8,128,8192]{2,1,0:T(8,128)(2,1)} %bitcast.21, bf16[8,128,8192]{2,1,0:T(8,128)(2,1)} %bitcast.22, f32[8,8,8192]{2,1,0:T(8,128)S(1)} %bitcast.13), custom_call_target="tpu_custom_call" | custom-call | tf_op jit(solution)/shard_map/left/pallas_call | solution.py:213
  15.6 6.2 %copy-done = bf16[8,128,8192]{2,1,0:T(8,128)(2,1)} copy-done((bf16[8,128,8192]{2,1,0:T(8,128)(2,1)}, bf16[8,128,8192]{2,1,0:T(8,128)(2,1)S(1)}, u32[]{:S(2)}) %copy-start) | copy-done | bytes 16777240
  21.7 6.2 %copy-done.3 = bf16[8,128,8192]{2,1,0:T(8,128)(2,1)} copy-done((bf16[8,128,8192]{2,1,0:T(8,128)(2,1)}, bf16[8,128,8192]{2,1,0:T(8,128)(2,1)S(1)}, u32[]{:S(2)}) %copy-start.3) | copy-done | bytes 16777240
  27.9 5.0 %collective-permute-start.2 = (f32[8,8,128]{2,1,0:T(8,128)S(1)}, f32[8,8,128]{2,1,0:T(8,128)S(1)}, u32[]{:S(2)}, u32[]{:S(2)}) collective-permute-start(f32[8,8,128]{2,1,0:T(8,128)S(1)} %get-tuple-element.17.refs_0_), channel_id=1, source_target_pairs={{0,24},{8,16},{16,8},{24,0},{1,25},{9,17},{17,9},{25,1},{2,26},{10... | collective-permute-start | bytes 98312 | tf_op jit(solution)/shard_map/ppermute | solution.py:207
  33.5 1.3 collective-permute-done.2.refs_3_
  34.8 2.9 %collective-permute-done.1.refs_2_ = f32[8,8,128]{2,1,0:T(8,128)S(1)} collective-permute-done((f32[8,8,128]{2,1,0:T(8,128)S(1)}, f32[8,8,128]{2,1,0:T(8,128)S(1)}, u32[]{:S(2)}, u32[]{:S(2)}) %collective-permute-start.1) | collective-permute-done | bytes 32800 | tf_op jit(solution)/shard_map/ppermute | solution.py:207
  37.7 5.8 %copy-done.1 = bf16[8,128,8192]{2,1,0:T(8,128)(2,1)S(1)} copy-done((bf16[8,128,8192]{2,1,0:T(8,128)(2,1)S(1)}, bf16[8,128,8192]{2,1,0:T(8,128)(2,1)}, u32[]{:S(2)}) %copy-start.1) | copy-done | bytes 16777240
  43.5 5.8 %copy-done.4 = bf16[8,128,8192]{2,1,0:T(8,128)(2,1)S(1)} copy-done((bf16[8,128,8192]{2,1,0:T(8,128)(2,1)S(1)}, bf16[8,128,8192]{2,1,0:T(8,128)(2,1)}, u32[]{:S(2)}) %copy-start.4) | copy-done | bytes 16777240
  49.3 9.5 %right.1 = (f32[8,8,128]{2,1,0:T(8,128)S(1)}, f32[8,128]{1,0:T(8,128)S(1)}, f32[16,16,8,128]{3,2,1,0:T(8,128)S(1)}, f32[16,16,8,128]{3,2,1,0:T(8,128)S(1)}) custom-call(s32[1]{0:T(128)} %bitcast.me_ref, bf16[8,128,8192]{2,1,0:T(8,128)(2,1)S(1)} %copy-done.1, bf16[8,128,8192]{2,1,0:T(8,128)(2,1)S(1)} %copy-done.4, ...), custom_call_target="tpu_custom_call" | custom-call | tf_op jit(solution)/shard_map/right/pallas_call | solution.py:234
  58.8 2.6 %collective-permute-done.7 = f32[16,16,8,128]{3,2,1,0:T(8,128)S(1)} collective-permute-done((f32[16,16,8,128]{3,2,1,0:T(8,128)S(1)}, f32[16,16,8,128]{3,2,1,0:T(8,128)S(1)}, u32[]{:S(2)}, u32[]{:S(2)}) %collective-permute-start.7) | collective-permute-done | bytes 1048608 | tf_op jit(solution)/shard_map/ppermute | solution.py:207
  61.6 2.5 %collective-permute-start.10 = (f32[4,16,8,128]{3,2,1,0:T(8,128)S(1)}, f32[4,16,8,128]{3,2,1,0:T(8,128)S(1)}, u32[]{:S(2)}, u32[]{:S(2)}) collective-permute-start(f32[4,16,8,128]{3,2,1,0:T(8,128)S(1)} %get-tuple-element.28), channel_id=1, source_target_pairs={{0,6},{1,7},{2,4},{3,5},{4,2},{5,3},{6,0},{7,1},{8,14},{9,15},{10,... | collective-permute-start | bytes 786440 | tf_op jit(solution)/shard_map/ppermute | solution.py:207
  65.2 1.2 collective-permute-done.3
  66.3 2.5 %collective-permute-start.6 = (f32[8,128]{1,0:T(8,128)S(1)}, f32[8,128]{1,0:T(8,128)S(1)}, u32[]{:S(2)}, u32[]{:S(2)}) collective-permute-start(f32[8,128]{1,0:T(8,128)S(1)} %add.108), channel_id=1, source_target_pairs={{0,6},{1,7},{2,4},{3,5},{4,2},{5,3},{6,0},{7,1},{8,14},{9,15},{10,... | collective-permute-start | bytes 12296 | tf_op jit(solution)/shard_map/ppermute | solution.py:207
  69.3 2.5 %collective-permute-done.10 = f32[4,16,8,128]{3,2,1,0:T(8,128)S(1)} collective-permute-done((f32[4,16,8,128]{3,2,1,0:T(8,128)S(1)}, f32[4,16,8,128]{3,2,1,0:T(8,128)S(1)}, u32[]{:S(2)}, u32[]{:S(2)}) %collective-permute-start.10) | collective-permute-done | bytes 262176 | tf_op jit(solution)/shard_map/ppermute | solution.py:207
  71.8 1.5 %collective-permute-start.4 = (f32[8,128]{1,0:T(8,128)S(1)}, f32[8,128]{1,0:T(8,128)S(1)}, u32[]{:S(2)}, u32[]{:S(2)}) collective-permute-start(f32[8,128]{1,0:T(8,128)S(1)} %add.108), channel_id=1, source_target_pairs={{0,2},{1,3},{2,0},{3,1},{4,6},{5,7},{6,4},{7,5},{8,10},{9,11},{10,... | collective-permute-start | bytes 12296 | tf_op jit(solution)/shard_map/ppermute | solution.py:207
  73.3 3.4 %collective-permute-done.9 = f32[4,16,8,128]{3,2,1,0:T(8,128)S(1)} collective-permute-done((f32[4,16,8,128]{3,2,1,0:T(8,128)S(1)}, f32[4,16,8,128]{3,2,1,0:T(8,128)S(1)}, u32[]{:S(2)}, u32[]{:S(2)}) %collective-permute-start.9) | collective-permute-done | bytes 262176 | tf_op jit(solution)/shard_map/ppermute | solution.py:207
  76.8 1.5 %collective-permute-start.13 = (f32[1,16,8,128]{3,2,1,0:T(8,128)S(1)}, f32[1,16,8,128]{3,2,1,0:T(8,128)S(1)}, u32[]{:S(2)}, u32[]{:S(2)}) collective-permute-start(f32[1,16,8,128]{3,2,1,0:T(8,128)S(1)} %get-tuple-element.31), channel_id=1, source_target_pairs={{0,24},{8,16},{16,8},{24,0},{1,25},{9,17},{17,9},{25,1},{2,26},{10... | collective-permute-start | bytes 196616 | tf_op jit(solution)/shard_map/ppermute | solution.py:207
  79.0 2.3 %collective-permute-start.11 = (f32[1,16,8,128]{3,2,1,0:T(8,128)S(1)}, f32[1,16,8,128]{3,2,1,0:T(8,128)S(1)}, u32[]{:S(2)}, u32[]{:S(2)}) collective-permute-start(f32[1,16,8,128]{3,2,1,0:T(8,128)S(1)} %get-tuple-element.33), channel_id=1, source_target_pairs={{0,8},{8,0},{16,24},{24,16},{1,9},{9,1},{17,25},{25,17},{2,10},{10... | collective-permute-start | bytes 196616 | tf_op jit(solution)/shard_map/ppermute | solution.py:207
  81.3 2.4 %collective-permute-done.13 = f32[1,16,8,128]{3,2,1,0:T(8,128)S(1)} collective-permute-done((f32[1,16,8,128]{3,2,1,0:T(8,128)S(1)}, f32[1,16,8,128]{3,2,1,0:T(8,128)S(1)}, u32[]{:S(2)}, u32[]{:S(2)}) %collective-permute-start.13) | collective-permute-done | bytes 65568 | tf_op jit(solution)/shard_map/ppermute | solution.py:207
  83.7 1.7 %collective-permute-done.12 = f32[1,16,8,128]{3,2,1,0:T(8,128)S(1)} collective-permute-done((f32[1,16,8,128]{3,2,1,0:T(8,128)S(1)}, f32[1,16,8,128]{3,2,1,0:T(8,128)S(1)}, u32[]{:S(2)}, u32[]{:S(2)}) %collective-permute-start.12) | collective-permute-done | bytes 65568 | tf_op jit(solution)/shard_map/ppermute | solution.py:207
  85.6 2.6 %collective-permute-start.16 = (f32[1,16,8,128]{3,2,1,0:T(8,128)S(1)}, f32[1,16,8,128]{3,2,1,0:T(8,128)S(1)}, u32[]{:S(2)}, u32[]{:S(2)}) collective-permute-start(f32[1,16,8,128]{3,2,1,0:T(8,128)S(1)} %bitcast.17), channel_id=1, source_target_pairs={{0,24},{8,16},{16,8},{24,0},{1,25},{9,17},{17,9},{25,1},{2,26},{10... | collective-permute-start | bytes 196616 | tf_op jit(solution)/shard_map/ppermute | solution.py:207
  88.2 1.9 %collective-permute-start.14 = (f32[1,16,8,128]{3,2,1,0:T(8,128)S(1)}, f32[1,16,8,128]{3,2,1,0:T(8,128)S(1)}, u32[]{:S(2)}, u32[]{:S(2)}) collective-permute-start(f32[1,16,8,128]{3,2,1,0:T(8,128)S(1)} %bitcast.19), channel_id=1, source_target_pairs={{0,8},{8,0},{16,24},{24,16},{1,9},{9,1},{17,25},{25,17},{2,10},{10... | collective-permute-start | bytes 196616 | tf_op jit(solution)/shard_map/ppermute | solution.py:207
  90.1 2.2 %collective-permute-done.16 = f32[1,16,8,128]{3,2,1,0:T(8,128)S(1)} collective-permute-done((f32[1,16,8,128]{3,2,1,0:T(8,128)S(1)}, f32[1,16,8,128]{3,2,1,0:T(8,128)S(1)}, u32[]{:S(2)}, u32[]{:S(2)}) %collective-permute-start.16) | collective-permute-done | bytes 65568 | tf_op jit(solution)/shard_map/ppermute | solution.py:207
  92.3 2.0 %collective-permute-done.15 = f32[1,16,8,128]{3,2,1,0:T(8,128)S(1)} collective-permute-done((f32[1,16,8,128]{3,2,1,0:T(8,128)S(1)}, f32[1,16,8,128]{3,2,1,0:T(8,128)S(1)}, u32[]{:S(2)}, u32[]{:S(2)}) %collective-permute-start.15) | collective-permute-done | bytes 65568 | tf_op jit(solution)/shard_map/ppermute | solution.py:207
  94.3 1.3 collective-permute-start.19
  95.6 1.7 %collective-permute-start.18 = (f32[4,16,8,128]{3,2,1,0:T(8,128)S(1)}, f32[4,16,8,128]{3,2,1,0:T(8,128)S(1)}, u32[]{:S(2)}, u32[]{:S(2)}) collective-permute-start(f32[4,16,8,128]{3,2,1,0:T(8,128)S(1)} %pad_maximum_fusion.refs_0_), channel_id=1, source_target_pairs={{0,4},{1,5},{2,6},{3,7},{4,0},{5,1},{6,2},{7,3},{8,12},{9,13},{10,... | collective-permute-start | bytes 786440 | tf_op jit(solution)/shard_map/ppermute | solution.py:207
  97.9 6.6 %collective-permute-done.19.refs_3_ = f32[4,16,8,128]{3,2,1,0:T(8,128)S(1)} collective-permute-done((f32[4,16,8,128]{3,2,1,0:T(8,128)S(1)}, f32[4,16,8,128]{3,2,1,0:T(8,128)S(1)}, u32[]{:S(2)}, u32[]{:S(2)}) %collective-permute-start.19) | collective-permute-done | bytes 262176 | tf_op jit(solution)/shard_map/ppermute | solution.py:207
  104.5 4.5 %collective-permute-done.18.refs_2_ = f32[4,16,8,128]{3,2,1,0:T(8,128)S(1)} collective-permute-done((f32[4,16,8,128]{3,2,1,0:T(8,128)S(1)}, f32[4,16,8,128]{3,2,1,0:T(8,128)S(1)}, u32[]{:S(2)}, u32[]{:S(2)}) %collective-permute-start.18) | collective-permute-done | bytes 262176 | tf_op jit(solution)/shard_map/ppermute | solution.py:207
  110.9 5.8 %copy-done.2 = bf16[8,128,8192]{2,1,0:T(8,128)(2,1)S(1)} copy-done((bf16[8,128,8192]{2,1,0:T(8,128)(2,1)S(1)}, bf16[8,128,8192]{2,1,0:T(8,128)(2,1)}, u32[]{:S(2)}) %copy-start.2) | copy-done | bytes 16777240
  116.7 5.8 %copy-done.5 = bf16[8,128,8192]{2,1,0:T(8,128)(2,1)S(1)} copy-done((bf16[8,128,8192]{2,1,0:T(8,128)(2,1)S(1)}, bf16[8,128,8192]{2,1,0:T(8,128)(2,1)}, u32[]{:S(2)}) %copy-start.5) | copy-done | bytes 16777240
  122.5 20.3 %out.1 = (bf16[8,128,8192]{2,1,0:T(8,128)(2,1)}, f32[8,128,8192]{2,1,0:T(8,128)}, f32[8,8,8192]{2,1,0:T(8,128)}) custom-call(s32[1]{0:T(128)} %bitcast.me_ref, bf16[8,128,8192]{2,1,0:T(8,128)(2,1)S(1)} %copy-done.2, bf16[8,128,8192]{2,1,0:T(8,128)(2,1)S(1)} %copy-done.5, f32[8,8,128]{2,1,0:T(8,128)S(1)} %get-tuple-element.18.sum_ref, ...), custom_call_target="tpu_custom_call" | custom-call | tf_op jit(solution)/shard_map/out/pallas_call | solution.py:284
  (39 shorter events, 5.9 us)
Async XLA Ops:
  0.6 1.6 %copy-start.6 = (f32[4,2,8,8192]{3,2,1,0:T(8,128)S(1)}, f32[4,2,8,8192]{3,2,1,0:T(8,128)}, u32[]{:S(2)}) copy-start(f32[4,2,8,8192]{3,2,1,0:T(8,128)} %param.5) | copy-start | bytes 6291460
  15.6 6.2 %copy-start = (bf16[8,128,8192]{2,1,0:T(8,128)(2,1)}, bf16[8,128,8192]{2,1,0:T(8,128)(2,1)S(1)}, u32[]{:S(2)}) copy-start(bf16[8,128,8192]{2,1,0:T(8,128)(2,1)S(1)} %get-tuple-element.15.g_ref) | copy-start | bytes 50331652
  21.7 6.2 %copy-start.3 = (bf16[8,128,8192]{2,1,0:T(8,128)(2,1)}, bf16[8,128,8192]{2,1,0:T(8,128)(2,1)S(1)}, u32[]{:S(2)}) copy-start(bf16[8,128,8192]{2,1,0:T(8,128)(2,1)S(1)} %get-tuple-element.16.e_ref) | copy-start | bytes 50331652
  27.9 6.9 %collective-permute-start.2 = (f32[8,8,128]{2,1,0:T(8,128)S(1)}, f32[8,8,128]{2,1,0:T(8,128)S(1)}, u32[]{:S(2)}, u32[]{:S(2)}) collective-permute-start(f32[8,8,128]{2,1,0:T(8,128)S(1)} %get-tuple-element.17.refs_0_), channel_id=1, source_target_pairs={{0,24},{8,16},{16,8},{24,0},{1,25},{9,17},{17,9},{25,1},{2,26},{10... | collective-permute-start | bytes 98312 | tf_op jit(solution)/shard_map/ppermute | solution.py:207
  32.9 4.8 %collective-permute-start.1 = (f32[8,8,128]{2,1,0:T(8,128)S(1)}, f32[8,8,128]{2,1,0:T(8,128)S(1)}, u32[]{:S(2)}, u32[]{:S(2)}) collective-permute-start(f32[8,8,128]{2,1,0:T(8,128)S(1)} %get-tuple-element.17.refs_0_), channel_id=1, source_target_pairs={{0,16},{8,24},{16,0},{24,8},{1,17},{9,25},{17,1},{25,9},{2,18},{10... | collective-permute-start | bytes 98312 | tf_op jit(solution)/shard_map/ppermute | solution.py:207
  32.9 4.8 %collective-permute-start = (f32[8,8,128]{2,1,0:T(8,128)S(1)}, f32[8,8,128]{2,1,0:T(8,128)S(1)}, u32[]{:S(2)}, u32[]{:S(2)}) collective-permute-start(f32[8,8,128]{2,1,0:T(8,128)S(1)} %get-tuple-element.17.refs_0_), channel_id=1, source_target_pairs={{0,8},{8,0},{16,24},{24,16},{1,9},{9,1},{17,25},{25,17},{2,10},{10... | collective-permute-start | bytes 98312 | tf_op jit(solution)/shard_map/ppermute | solution.py:207
  37.7 5.8 %copy-start.1 = (bf16[8,128,8192]{2,1,0:T(8,128)(2,1)S(1)}, bf16[8,128,8192]{2,1,0:T(8,128)(2,1)}, u32[]{:S(2)}) copy-start(bf16[8,128,8192]{2,1,0:T(8,128)(2,1)} %copy-done) | copy-start | bytes 50331652
  43.5 5.8 %copy-start.4 = (bf16[8,128,8192]{2,1,0:T(8,128)(2,1)S(1)}, bf16[8,128,8192]{2,1,0:T(8,128)(2,1)}, u32[]{:S(2)}) copy-start(bf16[8,128,8192]{2,1,0:T(8,128)(2,1)} %copy-done.3) | copy-start | bytes 50331652
  58.8 2.7 %collective-permute-start.7 = (f32[16,16,8,128]{3,2,1,0:T(8,128)S(1)}, f32[16,16,8,128]{3,2,1,0:T(8,128)S(1)}, u32[]{:S(2)}, u32[]{:S(2)}) collective-permute-start(f32[16,16,8,128]{3,2,1,0:T(8,128)S(1)} %get-tuple-element.21), channel_id=1, source_target_pairs={{0,1},{1,0},{2,3},{3,2},{4,5},{5,4},{6,7},{7,6},{8,9},{9,8},{10,11... | collective-permute-start | bytes 3145736 | tf_op jit(solution)/shard_map/ppermute | solution.py:207
  61.6 10.2 %collective-permute-start.10 = (f32[4,16,8,128]{3,2,1,0:T(8,128)S(1)}, f32[4,16,8,128]{3,2,1,0:T(8,128)S(1)}, u32[]{:S(2)}, u32[]{:S(2)}) collective-permute-start(f32[4,16,8,128]{3,2,1,0:T(8,128)S(1)} %get-tuple-element.28), channel_id=1, source_target_pairs={{0,6},{1,7},{2,4},{3,5},{4,2},{5,3},{6,0},{7,1},{8,14},{9,15},{10,... | collective-permute-start | bytes 786440 | tf_op jit(solution)/shard_map/ppermute | solution.py:207
  64.1 12.5 %collective-permute-start.9 = (f32[4,16,8,128]{3,2,1,0:T(8,128)S(1)}, f32[4,16,8,128]{3,2,1,0:T(8,128)S(1)}, u32[]{:S(2)}, u32[]{:S(2)}) collective-permute-start(f32[4,16,8,128]{3,2,1,0:T(8,128)S(1)} %get-tuple-element.29), channel_id=1, source_target_pairs={{0,4},{1,5},{2,6},{3,7},{4,0},{5,1},{6,2},{7,3},{8,12},{9,13},{10,... | collective-permute-start | bytes 786440 | tf_op jit(solution)/shard_map/ppermute | solution.py:207
  64.6 12.1 %collective-permute-start.8 = (f32[4,16,8,128]{3,2,1,0:T(8,128)S(1)}, f32[4,16,8,128]{3,2,1,0:T(8,128)S(1)}, u32[]{:S(2)}, u32[]{:S(2)}) collective-permute-start(f32[4,16,8,128]{3,2,1,0:T(8,128)S(1)} %get-tuple-element.30), channel_id=1, source_target_pairs={{0,2},{1,3},{2,0},{3,1},{4,6},{5,7},{6,4},{7,5},{8,10},{9,11},{10,... | collective-permute-start | bytes 786440 | tf_op jit(solution)/shard_map/ppermute | solution.py:207
  65.2 1.2 collective-permute-start.3
  66.3 12.6 %collective-permute-start.6 = (f32[8,128]{1,0:T(8,128)S(1)}, f32[8,128]{1,0:T(8,128)S(1)}, u32[]{:S(2)}, u32[]{:S(2)}) collective-permute-start(f32[8,128]{1,0:T(8,128)S(1)} %add.108), channel_id=1, source_target_pairs={{0,6},{1,7},{2,4},{3,5},{4,2},{5,3},{6,0},{7,1},{8,14},{9,15},{10,... | collective-permute-start | bytes 12296 | tf_op jit(solution)/shard_map/ppermute | solution.py:207
  68.8 12.5 %collective-permute-start.5 = (f32[8,128]{1,0:T(8,128)S(1)}, f32[8,128]{1,0:T(8,128)S(1)}, u32[]{:S(2)}, u32[]{:S(2)}) collective-permute-start(f32[8,128]{1,0:T(8,128)S(1)} %add.108), channel_id=1, source_target_pairs={{0,4},{1,5},{2,6},{3,7},{4,0},{5,1},{6,2},{7,3},{8,12},{9,13},{10,... | collective-permute-start | bytes 12296 | tf_op jit(solution)/shard_map/ppermute | solution.py:207
  71.8 9.5 %collective-permute-start.4 = (f32[8,128]{1,0:T(8,128)S(1)}, f32[8,128]{1,0:T(8,128)S(1)}, u32[]{:S(2)}, u32[]{:S(2)}) collective-permute-start(f32[8,128]{1,0:T(8,128)S(1)} %add.108), channel_id=1, source_target_pairs={{0,2},{1,3},{2,0},{3,1},{4,6},{5,7},{6,4},{7,5},{8,10},{9,11},{10,... | collective-permute-start | bytes 12296 | tf_op jit(solution)/shard_map/ppermute | solution.py:207
  76.8 6.9 %collective-permute-start.13 = (f32[1,16,8,128]{3,2,1,0:T(8,128)S(1)}, f32[1,16,8,128]{3,2,1,0:T(8,128)S(1)}, u32[]{:S(2)}, u32[]{:S(2)}) collective-permute-start(f32[1,16,8,128]{3,2,1,0:T(8,128)S(1)} %get-tuple-element.31), channel_id=1, source_target_pairs={{0,24},{8,16},{16,8},{24,0},{1,25},{9,17},{17,9},{25,1},{2,26},{10... | collective-permute-start | bytes 196616 | tf_op jit(solution)/shard_map/ppermute | solution.py:207
  78.3 7.0 %collective-permute-start.12 = (f32[1,16,8,128]{3,2,1,0:T(8,128)S(1)}, f32[1,16,8,128]{3,2,1,0:T(8,128)S(1)}, u32[]{:S(2)}, u32[]{:S(2)}) collective-permute-start(f32[1,16,8,128]{3,2,1,0:T(8,128)S(1)} %get-tuple-element.32), channel_id=1, source_target_pairs={{0,16},{8,24},{16,0},{24,8},{1,17},{9,25},{17,1},{25,9},{2,18},{10... | collective-permute-start | bytes 196616 | tf_op jit(solution)/shard_map/ppermute | solution.py:207
  79.0 6.4 %collective-permute-start.11 = (f32[1,16,8,128]{3,2,1,0:T(8,128)S(1)}, f32[1,16,8,128]{3,2,1,0:T(8,128)S(1)}, u32[]{:S(2)}, u32[]{:S(2)}) collective-permute-start(f32[1,16,8,128]{3,2,1,0:T(8,128)S(1)} %get-tuple-element.33), channel_id=1, source_target_pairs={{0,8},{8,0},{16,24},{24,16},{1,9},{9,1},{17,25},{25,17},{2,10},{10... | collective-permute-start | bytes 196616 | tf_op jit(solution)/shard_map/ppermute | solution.py:207
  85.6 6.7 %collective-permute-start.16 = (f32[1,16,8,128]{3,2,1,0:T(8,128)S(1)}, f32[1,16,8,128]{3,2,1,0:T(8,128)S(1)}, u32[]{:S(2)}, u32[]{:S(2)}) collective-permute-start(f32[1,16,8,128]{3,2,1,0:T(8,128)S(1)} %bitcast.17), channel_id=1, source_target_pairs={{0,24},{8,16},{16,8},{24,0},{1,25},{9,17},{17,9},{25,1},{2,26},{10... | collective-permute-start | bytes 196616 | tf_op jit(solution)/shard_map/ppermute | solution.py:207
  88.2 6.0 %collective-permute-start.15 = (f32[1,16,8,128]{3,2,1,0:T(8,128)S(1)}, f32[1,16,8,128]{3,2,1,0:T(8,128)S(1)}, u32[]{:S(2)}, u32[]{:S(2)}) collective-permute-start(f32[1,16,8,128]{3,2,1,0:T(8,128)S(1)} %bitcast.18), channel_id=1, source_target_pairs={{0,16},{8,24},{16,0},{24,8},{1,17},{9,25},{17,1},{25,9},{2,18},{10... | collective-permute-start | bytes 196616 | tf_op jit(solution)/shard_map/ppermute | solution.py:207
  88.2 6.0 %collective-permute-start.14 = (f32[1,16,8,128]{3,2,1,0:T(8,128)S(1)}, f32[1,16,8,128]{3,2,1,0:T(8,128)S(1)}, u32[]{:S(2)}, u32[]{:S(2)}) collective-permute-start(f32[1,16,8,128]{3,2,1,0:T(8,128)S(1)} %bitcast.19), channel_id=1, source_target_pairs={{0,8},{8,0},{16,24},{24,16},{1,9},{9,1},{17,25},{25,17},{2,10},{10... | collective-permute-start | bytes 196616 | tf_op jit(solution)/shard_map/ppermute | solution.py:207
  94.3 10.2 %collective-permute-start.19 = (f32[4,16,8,128]{3,2,1,0:T(8,128)S(1)}, f32[4,16,8,128]{3,2,1,0:T(8,128)S(1)}, u32[]{:S(2)}, u32[]{:S(2)}) collective-permute-start(f32[4,16,8,128]{3,2,1,0:T(8,128)S(1)} %pad_maximum_fusion.refs_0_), channel_id=1, source_target_pairs={{0,6},{1,7},{2,4},{3,5},{4,2},{5,3},{6,0},{7,1},{8,14},{9,15},{10,... | collective-permute-start | bytes 786440 | tf_op jit(solution)/shard_map/ppermute | solution.py:207
  95.6 13.4 %collective-permute-start.18 = (f32[4,16,8,128]{3,2,1,0:T(8,128)S(1)}, f32[4,16,8,128]{3,2,1,0:T(8,128)S(1)}, u32[]{:S(2)}, u32[]{:S(2)}) collective-permute-start(f32[4,16,8,128]{3,2,1,0:T(8,128)S(1)} %pad_maximum_fusion.refs_0_), channel_id=1, source_target_pairs={{0,4},{1,5},{2,6},{3,7},{4,0},{5,1},{6,2},{7,3},{8,12},{9,13},{10,... | collective-permute-start | bytes 786440 | tf_op jit(solution)/shard_map/ppermute | solution.py:207
  97.3 11.8 %collective-permute-start.17 = (f32[4,16,8,128]{3,2,1,0:T(8,128)S(1)}, f32[4,16,8,128]{3,2,1,0:T(8,128)S(1)}, u32[]{:S(2)}, u32[]{:S(2)}) collective-permute-start(f32[4,16,8,128]{3,2,1,0:T(8,128)S(1)} %pad_maximum_fusion.refs_0_), channel_id=1, source_target_pairs={{0,2},{1,3},{2,0},{3,1},{4,6},{5,7},{6,4},{7,5},{8,10},{9,11},{10,... | collective-permute-start | bytes 786440 | tf_op jit(solution)/shard_map/ppermute | solution.py:207
  97.9 11.7 %collective-permute-start.20 = (f32[4,16,8,128]{3,2,1,0:T(8,128)S(1)}, f32[4,16,8,128]{3,2,1,0:T(8,128)S(1)}, u32[]{:S(2)}, u32[]{:S(2)}) collective-permute-start(f32[4,16,8,128]{3,2,1,0:T(8,128)S(1)} %pad_maximum_fusion.refs_0_), channel_id=1, source_target_pairs={{0,1},{1,0},{2,3},{3,2},{4,5},{5,4},{6,7},{7,6},{8,9},{9,8},{10,11... | collective-permute-start | bytes 786440 | tf_op jit(solution)/shard_map/ppermute | solution.py:207
  104.5 5.1 %collective-permute-start.23 = (f32[4,16,8,128]{3,2,1,0:T(8,128)S(1)}, f32[4,16,8,128]{3,2,1,0:T(8,128)S(1)}, u32[]{:S(2)}, u32[]{:S(2)}) collective-permute-start(f32[4,16,8,128]{3,2,1,0:T(8,128)S(1)} %collective-permute-done.19.refs_3_), channel_id=1, source_target_pairs={{0,1},{1,0},{2,3},{3,2},{4,5},{5,4},{6,7},{7,6},{8,9},{9,8},{10,11... | collective-permute-start | bytes 786440 | tf_op jit(solution)/shard_map/ppermute | solution.py:207
  109.0 1.5 %collective-permute-start.22 = (f32[4,16,8,128]{3,2,1,0:T(8,128)S(1)}, f32[4,16,8,128]{3,2,1,0:T(8,128)S(1)}, u32[]{:S(2)}, u32[]{:S(2)}) collective-permute-start(f32[4,16,8,128]{3,2,1,0:T(8,128)S(1)} %collective-permute-done.18.refs_2_), channel_id=1, source_target_pairs={{0,1},{1,0},{2,3},{3,2},{4,5},{5,4},{6,7},{7,6},{8,9},{9,8},{10,11... | collective-permute-start | bytes 786440 | tf_op jit(solution)/shard_map/ppermute | solution.py:207
  109.1 1.8 %collective-permute-start.21 = (f32[4,16,8,128]{3,2,1,0:T(8,128)S(1)}, f32[4,16,8,128]{3,2,1,0:T(8,128)S(1)}, u32[]{:S(2)}, u32[]{:S(2)}) collective-permute-start(f32[4,16,8,128]{3,2,1,0:T(8,128)S(1)} %collective-permute-done.17.refs_1_), channel_id=1, source_target_pairs={{0,1},{1,0},{2,3},{3,2},{4,5},{5,4},{6,7},{7,6},{8,9},{9,8},{10,11... | collective-permute-start | bytes 786440 | tf_op jit(solution)/shard_map/ppermute | solution.py:207
  110.9 5.8 %copy-start.2 = (bf16[8,128,8192]{2,1,0:T(8,128)(2,1)S(1)}, bf16[8,128,8192]{2,1,0:T(8,128)(2,1)}, u32[]{:S(2)}) copy-start(bf16[8,128,8192]{2,1,0:T(8,128)(2,1)} %copy-done) | copy-start | bytes 50331652
  116.7 5.8 %copy-start.5 = (bf16[8,128,8192]{2,1,0:T(8,128)(2,1)S(1)}, bf16[8,128,8192]{2,1,0:T(8,128)(2,1)}, u32[]{:S(2)}) copy-start(bf16[8,128,8192]{2,1,0:T(8,128)(2,1)} %copy-done.3) | copy-start | bytes 50331652

commit v2 on v0

v2 whole, which is shorter than its diff:
```python
import functools

import jax
import jax.numpy as jnp
from jax import lax
from jax.experimental import pallas as pl
from jax.experimental.pallas import tpu as pltpu
from jax.sharding import PartitionSpec as P

F32 = jnp.float32
BF16 = jnp.bfloat16
LANES = 128
MIB = 1 << 20


def split3(x):
    hi = x.astype(BF16).astype(F32)
    rest = x - hi
    mid = rest.astype(BF16).astype(F32)
    low = (rest - mid).astype(BF16).astype(F32)
    return hi, mid, low


def tree_sum(terms):
    terms = list(terms)
    while len(terms) > 1:
        terms = [terms[i] + terms[i + 1] for i in range(0, len(terms), 2)]
    return terms[0]


def left_kernel(g_ref, e_ref, q_ref, p_out, total, *, splits):
    part = pl.program_id(1)
    rows = g_ref.shape[1]
    rank = q_ref.shape[1]
    basis = jnp.concatenate(split3(q_ref[0]), axis=0).astype(BF16)
    both = jnp.concatenate([g_ref[0], e_ref[0]], axis=0)
    here = lax.dot_general(both, basis, (((1,), (1,)), ((), ())), preferred_element_type=F32)

    @pl.when(part == 0)
    def _():
        total[...] = here

    @pl.when(part > 0)
    def _():
        total[...] += here

    @pl.when(part == splits - 1)
    def _():
        whole = (total[:rows] + total[rows:]).T
        p_out[0] = whole[:rank] + (whole[rank : 2 * rank] + whole[2 * rank :])


def right_kernel(core_ref, g_ref, e_ref, *refs, flip, splits):
    p_refs, (sum_out, out, left) = refs[:-3], refs[-3:]
    i = pl.program_id(0)
    part = pl.program_id(1)
    count, rank, _ = sum_out.shape
    half = out.shape[0] - 1
    tiles = g_ref.shape[2] // LANES

    @pl.when((i == 0) & (part == 0))
    def _():
        p_sum = tree_sum([r[...] for r in p_refs])
        sum_out[...] = p_sum
        lane = lax.broadcasted_iota(jnp.int32, (rank, LANES), 1)
        gram = jnp.zeros((rank, LANES), F32)
        for m in range(count):
            one = p_sum[m]
            for j in range(rank):
                column = jnp.sum(one * one[j : j + 1], axis=1, keepdims=True)
                gram = jnp.where(lane == j * count + m, column, gram)
            terms = jnp.concatenate(split3(one), axis=0)
            left[m] = jnp.concatenate([terms, terms], axis=1).astype(BF16)
        out[half] = gram

    m = jnp.bitwise_xor(core_ref[0], flip) * (count // 2) + i
    both = jnp.concatenate([g_ref[0], e_ref[0]], axis=0)
    product = jnp.dot(left[m], both, preferred_element_type=F32)
    product = product[:rank] + (product[rank : 2 * rank] + product[2 * rank :])
    first = (i * splits + part) * tiles
    for t in range(tiles):
        out[first + t] = product[:, t * LANES : (t + 1) * LANES]


def fold_kernel(at_ref, *refs, count, extra):
    terms, outs = refs[: len(refs) - count - extra], refs[len(refs) - count - extra :]
    size = terms[0].shape[0] - 1
    each = size // count
    last = tree_sum([r[size] for r in terms])
    for k in range(count):
        start = pl.multiple_of(jnp.bitwise_xor(at_ref[0], k) * each, each)
        here = pl.ds(start, each)
        outs[k][:each] = tree_sum([r[here] for r in terms])
        if not extra:
            outs[k][each] = last
    if extra:
        outs[count][...] = last


def join_kernel(at_ref, *refs):
    pieces, out = refs[:-1], refs[-1]
    each = pieces[0].shape[0]
    for k, piece in enumerate(pieces):
        start = pl.multiple_of(jnp.bitwise_xor(at_ref[0], k) * each, each)
        out[pl.ds(start, each)] = piece[...]


def invert(gram, matrices, rank):
    row = lax.broadcasted_iota(jnp.int32, (rank, LANES), 0)
    lane = lax.broadcasted_iota(jnp.int32, (rank, LANES), 1)
    used = lane < matrices
    unit = [jnp.where(row == j, 1.0, 0.0).astype(F32) for j in range(rank)]
    cols = [
        jnp.where(used, gram if j == 0 else pltpu.roll(gram, LANES - j * matrices, 1), unit[j]) for j in range(rank)
    ]
    inverse = list(unit)
    scale = jnp.ones((rank, LANES), F32)
    for k in range(rank):
        pivot = jnp.broadcast_to(cols[k][k : k + 1], (rank, LANES))
        scale = jnp.where(row == k, 1.0 / jnp.sqrt(pivot), scale)
        factor = jnp.where(row > k, cols[k] / pivot, 0.0)
        for j in range(k + 1, rank):
            cols[j] = cols[j] - factor * cols[j][k : k + 1]
        for j in range(k + 1):
            inverse[j] = inverse[j] - factor * inverse[j][k : k + 1]
    return [scale * c for c in inverse]


def piece_kernel(at_ref, gram_ref, *refs, per, matrices):
    parts, (q_out, inv_out) = refs[:-2], refs[-2:]
    rank = gram_ref.shape[0]
    inverse = invert(gram_ref[...], matrices, rank)
    for j in range(rank):
        inv_out[j] = inverse[j]
    m = at_ref[0] // per
    lane = lax.broadcasted_iota(jnp.int32, (rank, LANES), 1)
    picked = [
        jnp.broadcast_to(jnp.sum(jnp.where(lane == m, c, 0.0), axis=1, keepdims=True), (rank, LANES)) / len(parts)
        for c in inverse
    ]
    for t in range(q_out.shape[0]):
        total = tree_sum([r[t] for r in parts])
        q_out[t] = sum(picked[j] * total[j : j + 1] for j in range(rank))


def out_kernel(core_ref, g_ref, e_ref, sum_ref, inv_ref, q_ref, *refs, flip):
    err_out, approx_out, q_out, token, left = refs[-5:]
    i = pl.program_id(0)
    rows, width = g_ref.shape[1:]
    count, rank, _ = sum_ref.shape

    @pl.when(pl.program_id(1) == 0)
    def _():
        m = jnp.bitwise_xor(core_ref[0], flip) * (count // 2) + i
        lane = lax.broadcasted_iota(jnp.int32, (rank, LANES), 1)
        one = sum_ref[m]
        orth = jnp.zeros((rank, rows), F32)
        for j in range(rank):
            weight = jnp.sum(jnp.where(lane == m, inv_ref[j], 0.0), axis=1, keepdims=True)
            orth = orth + weight * one[j : j + 1]
        hi = orth.astype(BF16).astype(F32)
        low = (orth - hi).astype(BF16).astype(F32)
        left[...] = jnp.concatenate([hi, low, hi], axis=0).T.astype(BF16)
        token[...] = inv_ref[0]

    step = min(width, 1024)
    for start in range(0, width, step):
        here = slice(start, start + step)
        right = jnp.concatenate([q_ref[t] for t in range(start // LANES, (start + step) // LANES)], axis=1)
        q_out[0, :, here] = right
        hi = right.astype(BF16).astype(F32)
        low = (right - hi).astype(BF16).astype(F32)
        terms = jnp.concatenate([hi, hi, low], axis=0).astype(BF16)
        approx = jnp.dot(left[...], terms, preferred_element_type=F32)
        approx_out[0, :, here] = approx
        merged = g_ref[0, :, here].astype(F32) + e_ref[0, :, here].astype(F32)
        err_out[0, :, here] = (merged - approx).astype(BF16)


VMEM = pl.BlockSpec(memory_space=pltpu.VMEM)
HBM = pl.BlockSpec(memory_space=pltpu.HBM)
SMEM = pl.BlockSpec(memory_space=pltpu.SMEM)
ANY = pl.BlockSpec(memory_space=pl.ANY)
CHUNKS = 2
LEFT_SPLITS = 2
RIGHT_SPLITS = 2
OUT_SPLITS = 4


def ordered(kernel, count, at=0):
    def call(*refs):
        kernel(*refs[:at], *refs[at + count :])

    return call


def limit(mib, **more):
    return pltpu.CompilerParams(vmem_limit_bytes=mib * MIB, **more)


def cost(moved, flops=0):
    return pl.CostEstimate(flops=flops, bytes_accessed=moved // 4, transcendentals=0)


def on_device(sizes, grad, error, q_prev):
    groups, shards = sizes
    _, layers, pair, rows, width = grad.shape
    matrices = layers * pair
    rank = q_prev.shape[2]
    plane = shards // 2
    pieces = groups * shards
    whole = (matrices, rows, width)
    count = matrices // CHUNKS
    half = count // 2 * width // LANES
    tiles = half // (plane * groups)
    in_bytes = 4 * rows * width
    out_bytes = in_bytes + 6 * rows * width

    shard = lax.axis_index("shard")
    core = lax.rem(shard, 2).reshape(1)
    chip = (shard // 2).reshape(1)
    group = lax.axis_index("dp").reshape(1)
    at = (core * plane + chip) * groups + group

    grads, errors, basis = [
        pltpu.with_memory_space_constraint(x, pltpu.HBM)
        for x in (grad.reshape(whole), error.reshape(whole), q_prev.reshape(matrices, rank, width))
    ]

    def tiled(*shape):
        return jax.ShapeDtypeStruct(shape + (rank, LANES), F32)

    def swap(x, name, k):
        size = sizes[0] if name == "dp" else sizes[1]
        return lax.ppermute(x, name, [(i, i ^ k) for i in range(size)])

    def small(kernel, out_shape, *args, name, after=()):
        return pl.pallas_call(
            ordered(kernel, len(after)),
            out_shape=out_shape,
            in_specs=[ANY] * len(after) + [SMEM] + [VMEM] * (len(args) - 1),
            out_specs=jax.tree.map(lambda _: VMEM, out_shape),
            compiler_params=limit(16),
            name=name,
        )(*after, *args)

    def left(first):
        wide = width // LEFT_SPLITS
        block = pl.BlockSpec((1, rows, wide), lambda m, s: (first + m, 0, s))
        return pl.pallas_call(
            functools.partial(left_kernel, splits=LEFT_SPLITS),
            grid=(count, LEFT_SPLITS),
            out_shape=jax.ShapeDtypeStruct((count, rank, rows), F32),
            in_specs=[block, block, pl.BlockSpec((1, rank, wide), lambda m, s: (first + m, 0, s))],
            out_specs=pl.BlockSpec((1, rank, rows), lambda m, s: (m, 0, 0)),
            scratch_shapes=[pltpu.VMEM((2 * rows, 3 * rank), F32)],
            compiler_params=limit(24, dimension_semantics=("arbitrary",) * 2),
            cost_estimate=cost(count * (in_bytes + 4 * rank * width)),
            name="left",
        )(grads, errors, basis)

    def right(first, flip, parts, after):
        wide = width // RIGHT_SPLITS
        block = pl.BlockSpec(
            (1, rows, wide), lambda m, s, core: (first + jnp.bitwise_xor(core[0], flip) * (count // 2) + m, 0, s)
        )
        return pl.pallas_call(
            ordered(functools.partial(right_kernel, flip=flip, splits=RIGHT_SPLITS), len(after), 1),
            out_shape=(jax.ShapeDtypeStruct((count, rank, rows), F32), tiled(half + 1)),
            grid_spec=pltpu.PrefetchScalarGridSpec(
                num_scalar_prefetch=1,
                grid=(count // 2, RIGHT_SPLITS),
                in_specs=[ANY] * len(after) + [block, block] + [VMEM] * groups,
                out_specs=(VMEM, VMEM),
                scratch_shapes=[pltpu.VMEM((count, 3 * rank, 2 * rows), BF16)],
            ),
            compiler_params=limit(24, dimension_semantics=("arbitrary",) * 2),
            cost_estimate=cost(count // 2 * in_bytes),
            name="right",
        )(core, *after, grads, errors, *parts)

    def out(first, flip, p_sum, inverse, right_factors, before, after):
        wide = width // OUT_SPLITS

        def place(m, s, core):
            return (first + jnp.bitwise_xor(core[0], flip) * (count // 2) + m, 0, s)

        block = pl.BlockSpec((1, rows, wide), place)
        return pl.pallas_call(
            ordered(functools.partial(out_kernel, flip=flip), len(after), 1),
            out_shape=(
                jax.ShapeDtypeStruct(whole, BF16),
                jax.ShapeDtypeStruct(whole, F32),
                jax.ShapeDtypeStruct((matrices, rank, width), F32),
                tiled(),
            ),
            grid_spec=pltpu.PrefetchScalarGridSpec(
                num_scalar_prefetch=1,
                grid=(count // 2, OUT_SPLITS),
                in_specs=[ANY] * len(after)
                + [block, block, VMEM, VMEM]
                + [pl.BlockSpec((wide // LANES, rank, LANES), lambda m, s, core: (m * OUT_SPLITS + s, 0, 0))]
                + [HBM] * len(before),
                out_specs=(block, block, pl.BlockSpec((1, rank, wide), place), VMEM),
                scratch_shapes=[pltpu.VMEM((rows, 3 * rank), BF16)],
            ),
            input_output_aliases={6 + len(after) + k: k for k in range(len(before))},
            compiler_params=limit(24, dimension_semantics=("arbitrary",) * 2),
            cost_estimate=cost(count // 2 * out_bytes),
            name="out",
        )(core, *after, grads, errors, p_sum, inverse, right_factors, *before)

    def spread(x, name, step, size):
        return [x] + [swap(x, name, k * step) for k in range(1, size)]

    def exchange(parts, name, step):
        return [parts[0]] + [swap(x, name, k * step) for k, x in enumerate(parts) if k]

    chunks = range(CHUNKS)
    starts = [c * count for c in chunks]
    own = [left(first) for first in starts]
    lefts = [spread(x, "dp", 1, groups) for x in own]
    sums, keeps, messages = [], [], []
    before = own[1:2]
    for c in chunks:
        p_sum, send = right(starts[c], 1, lefts[c], before)
        arrived = swap(send, "shard", 1)
        _, keep = right(starts[c], 0, lefts[c], [p_sum])
        sums.append(p_sum)
        keeps.append(keep)
        messages.append(
            small(
                functools.partial(fold_kernel, count=plane, extra=0),
                (tiled(half // plane + 1),) * plane,
                chip, keep, arrived, name="fold_plane",
            )
        )
        before = messages[-1][:1]
    def group_stage(c, after):
        *parts, gram = small(
            functools.partial(fold_kernel, count=groups, extra=1),
            (tiled(tiles),) * groups + (tiled(),),
            group, *exchange(messages[c], "shard", 2), name="fold_group", after=after,
        )
        return parts, gram

    folded = [group_stage(0, keeps[1:2])]
    inverses, rows_here, pieces_made = [], [], []
    before = [x[0] for x in messages[1:2]]
    for c in chunks:
        parts, gram = folded[c]
        piece, inverse = small(
            functools.partial(piece_kernel, per=pieces // count, matrices=count),
            (tiled(tiles), tiled(rank)),
            at, gram, *exchange(parts, "dp", 1), name="piece", after=before,
        )
        pieces_made.append(piece)
        if c + 1 < CHUNKS:
            folded.append(group_stage(c + 1, [piece]))
        before = [x[0][0] for x in folded[c + 1 : c + 2]]
        row = small(
            join_kernel, tiled(tiles * groups), group, *spread(piece, "dp", 1, groups), name="join_group", after=before
        )
        before = [row]
        inverses.append(inverse)
        rows_here.append(spread(row, "shard", 2, plane))
    results, done = (), pieces_made[1:2]
    for c in chunks:
        mine = small(join_kernel, tiled(half), chip, *rows_here[c], name="join_plane", after=done)
        following = [x[0] for x in rows_here[c + 1 : c + 2]]
        for flip, factors in enumerate((mine, swap(mine, "shard", 1))):
            *results, token = out(starts[c], flip, sums[c], inverses[c], factors, results, following)
            following, done = [], [token]
    error_out, approx, q_new = results
    return error_out.reshape(grad.shape), approx.reshape(layers, pair, rows, width), q_new.reshape(q_prev.shape)


def solution(mesh):
    sizes = (mesh.shape["dp"], mesh.shape["shard"])
    in_specs = (P("dp", None, None, "shard", None), P("dp", None, None, "shard", None), P())
    out_specs = (P("dp", None, None, "shard", None), P(None, None, "shard", None), P())
    return jax.shard_map(
        functools.partial(on_device, sizes), mesh=mesh, in_specs=in_specs, out_specs=out_specs, check_vma=False
    )
```

time: 477 us -> 149 us (0.31)
  blocking collectives: 210 us -> 0 us
  waiting for transfers between devices: 131 us -> 18.9 us
  matrix products: 94.1 us -> 0 us
  Pallas kernels: 0 us -> 85.5 us
  starting transfers between devices: 0.04 us -> 42.4 us
  other arithmetic: 26.6 us -> 0 us
  between operations: 14.2 us -> 0.88 us
    psum x17 -> x0, blocking collectives: 210 us -> none  [the longest x8 94.6 us: on_device(): norm = lax.psum(jnp.sum(column * column, axis=1), 'shard')]
    psum x1 -> x0, waiting for transfers between devices: 131 us -> none  [on_device(): total_q = lax.psum(local_q, ('dp', 'shard'))]
    dot_general x19 -> x0, matrix products: 94.1 us -> none  [the longest x1 37.9 us: on_device(): approx = jnp.einsum('mrk,mkd->mrd', p_orth, q_new, precision=highest)]
    pallas_call x0 -> x20, Pallas kernels: none -> 85.5 us  [the longest x4 43.3 us: out(): pl.pallas_call(ordered(functools.partial(out_kernel, flip=flip), len(afte...]
    ppermute x0 -> x34, starting transfers between devices: none -> 42.4 us  [swap(): return lax.ppermute(x, name, [(i, i ^ k) for i in range(size)])]
    add x1 -> x0, other arithmetic: 23.5 us -> none  [on_device(): grad.astype(jnp.float32) + error.astype(jnp.float32)]
    ppermute x0 -> x34, waiting for transfers between devices: none -> 18.9 us  [swap(): return lax.ppermute(x, name, [(i, i ^ k) for i in range(size)])]
  transfers between devices with their start and end apart: 1 -> 34, of which waited for: 1 -> 9; matrix products, arithmetic and copies ran while one was open for 0% -> 0% of each run, Pallas kernels for 0% -> 37%
where the time goes in v2:
time: 149 us; the launch traced here: 148 us
  Pallas kernels  85.5 us (57%)
  starting transfers between devices  42.4 us (28%)
  waiting for transfers between devices  18.9 us (13%)
    pallas_call x4, Pallas kernels, out(): pl.pallas_call(ordered(functools.partial(out_kernel, flip=flip), len(afte...  43.3 us
    ppermute x34, starting transfers between devices, swap(): return lax.ppermute(x, name, [(i, i ^ k) for i in range(size)])  42.4 us
    pallas_call x2, Pallas kernels, left(): pl.pallas_call(functools.partial(left_kernel, splits=LEFT_SPLITS), grid=(...  20.8 us
    pallas_call x4, Pallas kernels, right(): pl.pallas_call(ordered(functools.partial(right_kernel, flip=flip, splits=...  20.5 us
    ppermute x34, waiting for transfers between devices, swap(): return lax.ppermute(x, name, [(i, i ^ k) for i in range(size)])  18.9 us
  transfers between devices with their start and end apart: 34, of which 9 were waited for; matrix products, arithmetic and copies ran while one was open for 0% of the time, Pallas kernels for 37%

profile of v2, /device:TPU:0, one launch (start us, length us, event | category | flops | bytes accessed | tf_op | source)
XLA Modules:
  0.0 147.7 jit_solution(3272577642673320309)
XLA Ops:
  0.6 10.4 %left.3.refs_4_ = f32[4,8,128]{2,1,0:T(8,128)S(1)} custom-call(bf16[8,128,8192]{2,1,0:T(8,128)(2,1)} %bitcast.9, bf16[8,128,8192]{2,1,0:T(8,128)(2,1)} %bitcast.19, f32[8,8,8192]{2,1,0:T(8,128)} %bitcast.32), custom_call_target="tpu_custom_call" | custom-call | bytes 4456448 | tf_op jit(solution)/shard_map/left/pallas_call | solution.py:250
  11.1 3.1 %collective-permute-start = (f32[4,8,128]{2,1,0:T(8,128)S(1)}, f32[4,8,128]{2,1,0:T(8,128)S(1)}, u32[]{:S(2)}, u32[]{:S(2)}) collective-permute-start(f32[4,8,128]{2,1,0:T(8,128)S(1)} %left.3.refs_4_), channel_id=1, source_target_pairs={{0,8},{8,0},{16,24},{24,16},{1,9},{9,1},{17,25},{25,17},{2,10},{10... | collective-permute-start | bytes 49160 | tf_op jit(solution)/shard_map/ppermute | solution.py:235
  14.2 2.6 %collective-permute-start.1 = (f32[4,8,128]{2,1,0:T(8,128)S(1)}, f32[4,8,128]{2,1,0:T(8,128)S(1)}, u32[]{:S(2)}, u32[]{:S(2)}) collective-permute-start(f32[4,8,128]{2,1,0:T(8,128)S(1)} %left.3.refs_4_), channel_id=1, source_target_pairs={{0,16},{8,24},{16,0},{24,8},{1,17},{9,25},{17,1},{25,9},{2,18},{10... | collective-permute-start | bytes 49160 | tf_op jit(solution)/shard_map/ppermute | solution.py:235
  16.7 10.4 %left.2.refs_1_.refs_4_ = f32[4,8,128]{2,1,0:T(8,128)S(1)} custom-call(bf16[8,128,8192]{2,1,0:T(8,128)(2,1)} %bitcast.10, bf16[8,128,8192]{2,1,0:T(8,128)(2,1)} %bitcast.20, f32[8,8,8192]{2,1,0:T(8,128)} %bitcast.33), custom_call_target="tpu_custom_call" | custom-call | bytes 4456448 | tf_op jit(solution)/shard_map/left/pallas_call | solution.py:250
  27.2 4.9 %right.4 = (f32[4,8,128]{2,1,0:T(8,128)S(1)}, f32[129,8,128]{2,1,0:T(8,128)S(1)}) custom-call(s32[1]{0:T(128)} %bitcast.refs_0_, f32[4,8,128]{2,1,0:T(8,128)S(1)} %left.2.refs_1_.refs_4_, bf16[8,128,8192]{2,1,0:T(8,128)(2,1)} %bitcast.11, bf16[8,128,8192]{2,1,0:T(8,128)(2,1)} %bitcast.21, f32[4,8,128]{2,1,0:T(8,128)S(1)} %left.3.refs_4_, ...), custom_call_target="tpu_custom_call" | custom-call | bytes 2097152 | tf_op jit(solution)/shard_map/right/pallas_call | solution.py:267
  32.2 1.0 collective-permute-start.4
  33.2 3.5 %collective-permute-start.5 = (f32[4,8,128]{2,1,0:T(8,128)S(1)}, f32[4,8,128]{2,1,0:T(8,128)S(1)}, u32[]{:S(2)}, u32[]{:S(2)}) collective-permute-start(f32[4,8,128]{2,1,0:T(8,128)S(1)} %left.2.refs_1_.refs_4_), channel_id=1, source_target_pairs={{0,16},{8,24},{16,0},{24,8},{1,17},{9,25},{17,1},{25,9},{2,18},{10... | collective-permute-start | bytes 49160 | tf_op jit(solution)/shard_map/ppermute | solution.py:235
  36.7 5.3 %right.5 = (f32[4,8,128]{2,1,0:T(8,128)}, f32[129,8,128]{2,1,0:T(8,128)S(1)}) custom-call(s32[1]{0:T(128)} %bitcast.refs_0_, f32[4,8,128]{2,1,0:T(8,128)S(1)} %get-tuple-element.44.refs_1_.refs_4_.refs_3_, bf16[8,128,8192]{2,1,0:T(8,128)(2,1)} %bitcast.12, bf16[8,128,8192]{2,1,0:T(8,128)(2,1)} %bitcast.22, f32[4,8,128]{2,1,0:T(8,128)S(1)} %left.3.refs_4_, ...), custom_call_target="tpu_custom_call" | custom-call | bytes 2097152 | tf_op jit(solution)/shard_map/right/pallas_call | solution.py:267
  42.2 4.9 %right.6 = (f32[4,8,128]{2,1,0:T(8,128)S(1)}, f32[129,8,128]{2,1,0:T(8,128)S(1)}) custom-call(s32[1]{0:T(128)} %bitcast.refs_0_, f32[33,8,128]{2,1,0:T(8,128)S(1)} %get-tuple-element.47.refs_1_.refs_2_, bf16[8,128,8192]{2,1,0:T(8,128)(2,1)} %bitcast.13, bf16[8,128,8192]{2,1,0:T(8,128)(2,1)} %bitcast.23, f32[4,8,128]{2,1,0:T(8,128)S(1)} %left.2.refs_1_.refs_4_, ...), custom_call_target="tpu_custom_call" | custom-call | bytes 2097152 | tf_op jit(solution)/shard_map/right/pallas_call | solution.py:267
  47.2 2.6 %collective-permute-start.10 = (f32[33,8,128]{2,1,0:T(8,128)S(1)}, f32[33,8,128]{2,1,0:T(8,128)S(1)}, u32[]{:S(2)}, u32[]{:S(2)}) collective-permute-start(f32[33,8,128]{2,1,0:T(8,128)S(1)} %get-tuple-element.54), channel_id=1, source_target_pairs={{0,6},{1,7},{2,4},{3,5},{4,2},{5,3},{6,0},{7,1},{8,14},{9,15},{10,... | collective-permute-start | bytes 405512 | tf_op jit(solution)/shard_map/ppermute | solution.py:235
  50.7 5.3 %right.7 = (f32[4,8,128]{2,1,0:T(8,128)}, f32[129,8,128]{2,1,0:T(8,128)S(1)}) custom-call(s32[1]{0:T(128)} %bitcast.refs_0_, f32[4,8,128]{2,1,0:T(8,128)S(1)} %get-tuple-element.48.refs_1_.refs_3_, bf16[8,128,8192]{2,1,0:T(8,128)(2,1)} %bitcast.14, bf16[8,128,8192]{2,1,0:T(8,128)(2,1)} %bitcast.24, f32[4,8,128]{2,1,0:T(8,128)S(1)} %left.2.refs_1_.refs_4_, ...), custom_call_target="tpu_custom_call" | custom-call | bytes 2097152 | tf_op jit(solution)/shard_map/right/pallas_call | solution.py:267
  56.2 1.7 %collective-permute-start.14 = (f32[33,8,128]{2,1,0:T(8,128)S(1)}, f32[33,8,128]{2,1,0:T(8,128)S(1)}, u32[]{:S(2)}, u32[]{:S(2)}) collective-permute-start(f32[33,8,128]{2,1,0:T(8,128)S(1)} %get-tuple-element.61), channel_id=1, source_target_pairs={{0,2},{1,3},{2,0},{3,1},{4,6},{5,7},{6,4},{7,5},{8,10},{9,11},{10,... | collective-permute-start | bytes 405512 | tf_op jit(solution)/shard_map/ppermute | solution.py:235
  57.8 1.5 %collective-permute-start.15 = (f32[33,8,128]{2,1,0:T(8,128)S(1)}, f32[33,8,128]{2,1,0:T(8,128)S(1)}, u32[]{:S(2)}, u32[]{:S(2)}) collective-permute-start(f32[33,8,128]{2,1,0:T(8,128)S(1)} %get-tuple-element.62), channel_id=1, source_target_pairs={{0,4},{1,5},{2,6},{3,7},{4,0},{5,1},{6,2},{7,3},{8,12},{9,13},{10,... | collective-permute-start | bytes 405512 | tf_op jit(solution)/shard_map/ppermute | solution.py:235
  60.3 3.8 %collective-permute-start.12 = (f32[8,8,128]{2,1,0:T(8,128)S(1)}, f32[8,8,128]{2,1,0:T(8,128)S(1)}, u32[]{:S(2)}, u32[]{:S(2)}) collective-permute-start(f32[8,8,128]{2,1,0:T(8,128)S(1)} %get-tuple-element.58), channel_id=1, source_target_pairs={{0,16},{8,24},{16,0},{24,8},{1,17},{9,25},{17,1},{25,9},{2,18},{10... | collective-permute-start | bytes 98312 | tf_op jit(solution)/shard_map/ppermute | solution.py:235
  64.1 3.3 %collective-permute-start.13 = (f32[8,8,128]{2,1,0:T(8,128)S(1)}, f32[8,8,128]{2,1,0:T(8,128)S(1)}, u32[]{:S(2)}, u32[]{:S(2)}) collective-permute-start(f32[8,8,128]{2,1,0:T(8,128)S(1)} %get-tuple-element.59), channel_id=1, source_target_pairs={{0,24},{8,16},{16,8},{24,0},{1,25},{9,17},{17,9},{25,1},{2,26},{10... | collective-permute-start | bytes 98312 | tf_op jit(solution)/shard_map/ppermute | solution.py:235
  67.5 2.4 %collective-permute-done.13.refs_6_ = f32[8,8,128]{2,1,0:T(8,128)S(1)} collective-permute-done((f32[8,8,128]{2,1,0:T(8,128)S(1)}, f32[8,8,128]{2,1,0:T(8,128)S(1)}, u32[]{:S(2)}, u32[]{:S(2)}) %collective-permute-start.13) | collective-permute-done | bytes 32800 | tf_op jit(solution)/shard_map/ppermute | solution.py:235
  70.2 3.9 %collective-permute-start.18 = (f32[8,8,128]{2,1,0:T(8,128)S(1)}, f32[8,8,128]{2,1,0:T(8,128)S(1)}, u32[]{:S(2)}, u32[]{:S(2)}) collective-permute-start(f32[8,8,128]{2,1,0:T(8,128)S(1)} %get-tuple-element.60.refs_0_.refs_2_), channel_id=1, source_target_pairs={{0,16},{8,24},{16,0},{24,8},{1,17},{9,25},{17,1},{25,9},{2,18},{10... | collective-permute-start | bytes 98312 | tf_op jit(solution)/shard_map/ppermute | solution.py:235
  74.6 1.4 collective-permute-done.18.refs_4_
  76.0 4.2 %collective-permute-done.19.refs_5_ = f32[8,8,128]{2,1,0:T(8,128)S(1)} collective-permute-done((f32[8,8,128]{2,1,0:T(8,128)S(1)}, f32[8,8,128]{2,1,0:T(8,128)S(1)}, u32[]{:S(2)}, u32[]{:S(2)}) %collective-permute-start.19) | collective-permute-done | bytes 32800 | tf_op jit(solution)/shard_map/ppermute | solution.py:235
  80.2 1.5 %collective-permute-start.23 = (f32[32,8,128]{2,1,0:T(8,128)S(1)}, f32[32,8,128]{2,1,0:T(8,128)S(1)}, u32[]{:S(2)}, u32[]{:S(2)}) collective-permute-start(f32[32,8,128]{2,1,0:T(8,128)S(1)} %join_group.2.refs_0_.refs_2_), channel_id=1, source_target_pairs={{0,2},{1,3},{2,0},{3,1},{4,6},{5,7},{6,4},{7,5},{8,10},{9,11},{10,... | collective-permute-start | bytes 393224 | tf_op jit(solution)/shard_map/ppermute | solution.py:235
  81.7 1.5 %collective-permute-start.24 = (f32[32,8,128]{2,1,0:T(8,128)S(1)}, f32[32,8,128]{2,1,0:T(8,128)S(1)}, u32[]{:S(2)}, u32[]{:S(2)}) collective-permute-start(f32[32,8,128]{2,1,0:T(8,128)S(1)} %join_group.2.refs_0_.refs_2_), channel_id=1, source_target_pairs={{0,4},{1,5},{2,6},{3,7},{4,0},{5,1},{6,2},{7,3},{8,12},{9,13},{10,... | collective-permute-start | bytes 393224 | tf_op jit(solution)/shard_map/ppermute | solution.py:235
  84.4 3.2 %collective-permute-done.20.refs_4_ = f32[8,8,128]{2,1,0:T(8,128)S(1)} collective-permute-done((f32[8,8,128]{2,1,0:T(8,128)S(1)}, f32[8,8,128]{2,1,0:T(8,128)S(1)}, u32[]{:S(2)}, u32[]{:S(2)}) %collective-permute-start.20) | collective-permute-done | bytes 32800 | tf_op jit(solution)/shard_map/ppermute | solution.py:235
  88.6 4.8 %collective-permute-done.22.refs_6_ = f32[8,8,128]{2,1,0:T(8,128)S(1)} collective-permute-done((f32[8,8,128]{2,1,0:T(8,128)S(1)}, f32[8,8,128]{2,1,0:T(8,128)S(1)}, u32[]{:S(2)}, u32[]{:S(2)}) %collective-permute-start.22) | collective-permute-done | bytes 32800 | tf_op jit(solution)/shard_map/ppermute | solution.py:235
  93.9 1.0 collective-permute-start.28
  94.9 3.3 %collective-permute-start.29 = (f32[8,8,128]{2,1,0:T(8,128)S(1)}, f32[8,8,128]{2,1,0:T(8,128)S(1)}, u32[]{:S(2)}, u32[]{:S(2)}) collective-permute-start(f32[8,8,128]{2,1,0:T(8,128)S(1)} %get-tuple-element.71.refs_0_.refs_1_), channel_id=1, source_target_pairs={{0,24},{8,16},{16,8},{24,0},{1,25},{9,17},{17,9},{25,1},{2,26},{10... | collective-permute-start | bytes 98312 | tf_op jit(solution)/shard_map/ppermute | solution.py:235
  98.8 1.8 %collective-permute-done.29.refs_4_ = f32[8,8,128]{2,1,0:T(8,128)S(1)} collective-permute-done((f32[8,8,128]{2,1,0:T(8,128)S(1)}, f32[8,8,128]{2,1,0:T(8,128)S(1)}, u32[]{:S(2)}, u32[]{:S(2)}) %collective-permute-start.29) | collective-permute-done | bytes 32800 | tf_op jit(solution)/shard_map/ppermute | solution.py:235
  100.7 1.5 %collective-permute-start.30 = (f32[32,8,128]{2,1,0:T(8,128)S(1)}, f32[32,8,128]{2,1,0:T(8,128)S(1)}, u32[]{:S(2)}, u32[]{:S(2)}) collective-permute-start(f32[32,8,128]{2,1,0:T(8,128)S(1)} %join_group.3.refs_1_.refs_2_), channel_id=1, source_target_pairs={{0,2},{1,3},{2,0},{3,1},{4,6},{5,7},{6,4},{7,5},{8,10},{9,11},{10,... | collective-permute-start | bytes 393224 | tf_op jit(solution)/shard_map/ppermute | solution.py:235
  102.2 1.5 %collective-permute-start.31 = (f32[32,8,128]{2,1,0:T(8,128)S(1)}, f32[32,8,128]{2,1,0:T(8,128)S(1)}, u32[]{:S(2)}, u32[]{:S(2)}) collective-permute-start(f32[32,8,128]{2,1,0:T(8,128)S(1)} %join_group.3.refs_1_.refs_2_), channel_id=1, source_target_pairs={{0,4},{1,5},{2,6},{3,7},{4,0},{5,1},{6,2},{7,3},{8,12},{9,13},{10,... | collective-permute-start | bytes 393224 | tf_op jit(solution)/shard_map/ppermute | solution.py:235
  104.2 10.8 %out.4 = (bf16[8,128,8192]{2,1,0:T(8,128)(2,1)}, f32[8,128,8192]{2,1,0:T(8,128)}, f32[8,8,8192]{2,1,0:T(8,128)}, f32[8,128]{1,0:T(8,128)}) custom-call(s32[1]{0:T(128)} %bitcast.refs_0_, f32[32,8,128]{2,1,0:T(8,128)S(1)} %join_group.3.refs_1_.refs_2_, bf16[8,128,8192]{2,1,0:T(8,128)(2,1)} %bitcast.15, bf16[8,128,8192]{2,1,0:T(8,128)(2,1)} %bitcast.25, ...), custom_call_target="tpu_custom_call" | custom-call | bytes 5242880 | tf_op jit(solution)/shard_map/out/pallas_call | solution.py:289
  115.0 10.8 %out.5 = (bf16[8,128,8192]{2,1,0:T(8,128)(2,1)}, f32[8,128,8192]{2,1,0:T(8,128)}, f32[8,8,8192]{2,1,0:T(8,128)}, f32[8,128]{1,0:T(8,128)S(1)}) custom-call(s32[1]{0:T(128)} %bitcast.refs_0_, bf16[8,128,8192]{2,1,0:T(8,128)(2,1)} %bitcast.16, bf16[8,128,8192]{2,1,0:T(8,128)(2,1)} %bitcast.26, ...), custom_call_target="tpu_custom_call", output_to_operand_aliasing={{0}: (6, {}), {1}: (7, {}), {2}: (8, {})} | custom-call | bytes 5242880 | tf_op jit(solution)/shard_map/out/pallas_call | solution.py:289
  126.0 10.8 %out.6 = (bf16[8,128,8192]{2,1,0:T(8,128)(2,1)}, f32[8,128,8192]{2,1,0:T(8,128)}, f32[8,8,8192]{2,1,0:T(8,128)}, f32[8,128]{1,0:T(8,128)}) custom-call(s32[1]{0:T(128)} %bitcast.refs_0_, bf16[8,128,8192]{2,1,0:T(8,128)(2,1)} %bitcast.17, bf16[8,128,8192]{2,1,0:T(8,128)(2,1)} %bitcast.27, ...), custom_call_target="tpu_custom_call", output_to_operand_aliasing={{0}: (6, {}), {1}: (7, {}), {2}: (8, {})} | custom-call | bytes 5242880 | tf_op jit(solution)/shard_map/out/pallas_call | solution.py:289
  136.9 10.8 %out.7 = (bf16[8,128,8192]{2,1,0:T(8,128)(2,1)}, f32[8,128,8192]{2,1,0:T(8,128)}, f32[8,8,8192]{2,1,0:T(8,128)}, f32[8,128]{1,0:T(8,128)}) custom-call(s32[1]{0:T(128)} %bitcast.refs_0_, bf16[8,128,8192]{2,1,0:T(8,128)(2,1)} %bitcast.18, bf16[8,128,8192]{2,1,0:T(8,128)(2,1)} %bitcast.28, ...), custom_call_target="tpu_custom_call", output_to_operand_aliasing={{0}: (6, {}), {1}: (7, {}), {2}: (8, {})} | custom-call | bytes 5242880 | tf_op jit(solution)/shard_map/out/pallas_call | solution.py:289
  (56 shorter events, 6.8 us)
Async XLA Ops:
  11.1 16.1 %collective-permute-start = (f32[4,8,128]{2,1,0:T(8,128)S(1)}, f32[4,8,128]{2,1,0:T(8,128)S(1)}, u32[]{:S(2)}, u32[]{:S(2)}) collective-permute-start(f32[4,8,128]{2,1,0:T(8,128)S(1)} %left.3.refs_4_), channel_id=1, source_target_pairs={{0,8},{8,0},{16,24},{24,16},{1,9},{9,1},{17,25},{25,17},{2,10},{10... | collective-permute-start | bytes 49160 | tf_op jit(solution)/shard_map/ppermute | solution.py:235
  14.2 13.0 %collective-permute-start.1 = (f32[4,8,128]{2,1,0:T(8,128)S(1)}, f32[4,8,128]{2,1,0:T(8,128)S(1)}, u32[]{:S(2)}, u32[]{:S(2)}) collective-permute-start(f32[4,8,128]{2,1,0:T(8,128)S(1)} %left.3.refs_4_), channel_id=1, source_target_pairs={{0,16},{8,24},{16,0},{24,8},{1,17},{9,25},{17,1},{25,9},{2,18},{10... | collective-permute-start | bytes 49160 | tf_op jit(solution)/shard_map/ppermute | solution.py:235
  16.7 10.4 %collective-permute-start.2 = (f32[4,8,128]{2,1,0:T(8,128)S(1)}, f32[4,8,128]{2,1,0:T(8,128)S(1)}, u32[]{:S(2)}, u32[]{:S(2)}) collective-permute-start(f32[4,8,128]{2,1,0:T(8,128)S(1)} %left.3.refs_4_), channel_id=1, source_target_pairs={{0,24},{8,16},{16,8},{24,0},{1,25},{9,17},{17,9},{25,1},{2,26},{10... | collective-permute-start | bytes 49160 | tf_op jit(solution)/shard_map/ppermute | solution.py:235
  32.1 9.9 %collective-permute-start.3 = (f32[129,8,128]{2,1,0:T(8,128)S(1)}, f32[129,8,128]{2,1,0:T(8,128)S(1)}, u32[]{:S(2)}, u32[]{:S(2)}) collective-permute-start(f32[129,8,128]{2,1,0:T(8,128)S(1)} %get-tuple-element.46), channel_id=1, source_target_pairs={{0,1},{1,0},{2,3},{3,2},{4,5},{5,4},{6,7},{7,6},{8,9},{9,8},{10,11... | collective-permute-start | bytes 1585160 | tf_op jit(solution)/shard_map/ppermute | solution.py:235
  32.2 9.9 %collective-permute-start.4 = (f32[4,8,128]{2,1,0:T(8,128)S(1)}, f32[4,8,128]{2,1,0:T(8,128)S(1)}, u32[]{:S(2)}, u32[]{:S(2)}) collective-permute-start(f32[4,8,128]{2,1,0:T(8,128)S(1)} %left.2.refs_1_.refs_4_), channel_id=1, source_target_pairs={{0,8},{8,0},{16,24},{24,16},{1,9},{9,1},{17,25},{25,17},{2,10},{10... | collective-permute-start | bytes 49160 | tf_op jit(solution)/shard_map/ppermute | solution.py:235
  33.2 8.9 %collective-permute-start.5 = (f32[4,8,128]{2,1,0:T(8,128)S(1)}, f32[4,8,128]{2,1,0:T(8,128)S(1)}, u32[]{:S(2)}, u32[]{:S(2)}) collective-permute-start(f32[4,8,128]{2,1,0:T(8,128)S(1)} %left.2.refs_1_.refs_4_), channel_id=1, source_target_pairs={{0,16},{8,24},{16,0},{24,8},{1,17},{9,25},{17,1},{25,9},{2,18},{10... | collective-permute-start | bytes 49160 | tf_op jit(solution)/shard_map/ppermute | solution.py:235
  36.7 5.5 %collective-permute-start.6 = (f32[4,8,128]{2,1,0:T(8,128)S(1)}, f32[4,8,128]{2,1,0:T(8,128)S(1)}, u32[]{:S(2)}, u32[]{:S(2)}) collective-permute-start(f32[4,8,128]{2,1,0:T(8,128)S(1)} %left.2.refs_1_.refs_4_), channel_id=1, source_target_pairs={{0,24},{8,16},{16,8},{24,0},{1,25},{9,17},{17,9},{25,1},{2,26},{10... | collective-permute-start | bytes 49160 | tf_op jit(solution)/shard_map/ppermute | solution.py:235
  47.1 9.0 %collective-permute-start.7 = (f32[129,8,128]{2,1,0:T(8,128)S(1)}, f32[129,8,128]{2,1,0:T(8,128)S(1)}, u32[]{:S(2)}, u32[]{:S(2)}) collective-permute-start(f32[129,8,128]{2,1,0:T(8,128)S(1)} %get-tuple-element.50), channel_id=1, source_target_pairs={{0,1},{1,0},{2,3},{3,2},{4,5},{5,4},{6,7},{7,6},{8,9},{9,8},{10,11... | collective-permute-start | bytes 1585160 | tf_op jit(solution)/shard_map/ppermute | solution.py:235
  47.2 12.2 %collective-permute-start.10 = (f32[33,8,128]{2,1,0:T(8,128)S(1)}, f32[33,8,128]{2,1,0:T(8,128)S(1)}, u32[]{:S(2)}, u32[]{:S(2)}) collective-permute-start(f32[33,8,128]{2,1,0:T(8,128)S(1)} %get-tuple-element.54), channel_id=1, source_target_pairs={{0,6},{1,7},{2,4},{3,5},{4,2},{5,3},{6,0},{7,1},{8,14},{9,15},{10,... | collective-permute-start | bytes 405512 | tf_op jit(solution)/shard_map/ppermute | solution.py:235
  49.8 9.9 %collective-permute-start.8 = (f32[33,8,128]{2,1,0:T(8,128)S(1)}, f32[33,8,128]{2,1,0:T(8,128)S(1)}, u32[]{:S(2)}, u32[]{:S(2)}) collective-permute-start(f32[33,8,128]{2,1,0:T(8,128)S(1)} %get-tuple-element.52), channel_id=1, source_target_pairs={{0,2},{1,3},{2,0},{3,1},{4,6},{5,7},{6,4},{7,5},{8,10},{9,11},{10,... | collective-permute-start | bytes 405512 | tf_op jit(solution)/shard_map/ppermute | solution.py:235
  50.4 9.4 %collective-permute-start.9 = (f32[33,8,128]{2,1,0:T(8,128)S(1)}, f32[33,8,128]{2,1,0:T(8,128)S(1)}, u32[]{:S(2)}, u32[]{:S(2)}) collective-permute-start(f32[33,8,128]{2,1,0:T(8,128)S(1)} %get-tuple-element.53), channel_id=1, source_target_pairs={{0,4},{1,5},{2,6},{3,7},{4,0},{5,1},{6,2},{7,3},{8,12},{9,13},{10,... | collective-permute-start | bytes 405512 | tf_op jit(solution)/shard_map/ppermute | solution.py:235
  56.2 18.0 %collective-permute-start.14 = (f32[33,8,128]{2,1,0:T(8,128)S(1)}, f32[33,8,128]{2,1,0:T(8,128)S(1)}, u32[]{:S(2)}, u32[]{:S(2)}) collective-permute-start(f32[33,8,128]{2,1,0:T(8,128)S(1)} %get-tuple-element.61), channel_id=1, source_target_pairs={{0,2},{1,3},{2,0},{3,1},{4,6},{5,7},{6,4},{7,5},{8,10},{9,11},{10,... | collective-permute-start | bytes 405512 | tf_op jit(solution)/shard_map/ppermute | solution.py:235
  57.8 16.7 %collective-permute-start.15 = (f32[33,8,128]{2,1,0:T(8,128)S(1)}, f32[33,8,128]{2,1,0:T(8,128)S(1)}, u32[]{:S(2)}, u32[]{:S(2)}) collective-permute-start(f32[33,8,128]{2,1,0:T(8,128)S(1)} %get-tuple-element.62), channel_id=1, source_target_pairs={{0,4},{1,5},{2,6},{3,7},{4,0},{5,1},{6,2},{7,3},{8,12},{9,13},{10,... | collective-permute-start | bytes 405512 | tf_op jit(solution)/shard_map/ppermute | solution.py:235
  59.4 15.2 %collective-permute-start.16 = (f32[33,8,128]{2,1,0:T(8,128)S(1)}, f32[33,8,128]{2,1,0:T(8,128)S(1)}, u32[]{:S(2)}, u32[]{:S(2)}) collective-permute-start(f32[33,8,128]{2,1,0:T(8,128)S(1)} %get-tuple-element.63), channel_id=1, source_target_pairs={{0,6},{1,7},{2,4},{3,5},{4,2},{5,3},{6,0},{7,1},{8,14},{9,15},{10,... | collective-permute-start | bytes 405512 | tf_op jit(solution)/shard_map/ppermute | solution.py:235
  60.3 7.2 %collective-permute-start.12 = (f32[8,8,128]{2,1,0:T(8,128)S(1)}, f32[8,8,128]{2,1,0:T(8,128)S(1)}, u32[]{:S(2)}, u32[]{:S(2)}) collective-permute-start(f32[8,8,128]{2,1,0:T(8,128)S(1)} %get-tuple-element.58), channel_id=1, source_target_pairs={{0,16},{8,24},{16,0},{24,8},{1,17},{9,25},{17,1},{25,9},{2,18},{10... | collective-permute-start | bytes 98312 | tf_op jit(solution)/shard_map/ppermute | solution.py:235
  64.1 5.7 %collective-permute-start.13 = (f32[8,8,128]{2,1,0:T(8,128)S(1)}, f32[8,8,128]{2,1,0:T(8,128)S(1)}, u32[]{:S(2)}, u32[]{:S(2)}) collective-permute-start(f32[8,8,128]{2,1,0:T(8,128)S(1)} %get-tuple-element.59), channel_id=1, source_target_pairs={{0,24},{8,16},{16,8},{24,0},{1,25},{9,17},{17,9},{25,1},{2,26},{10... | collective-permute-start | bytes 98312 | tf_op jit(solution)/shard_map/ppermute | solution.py:235
  70.1 4.5 %collective-permute-start.17 = (f32[8,8,128]{2,1,0:T(8,128)S(1)}, f32[8,8,128]{2,1,0:T(8,128)S(1)}, u32[]{:S(2)}, u32[]{:S(2)}) collective-permute-start(f32[8,8,128]{2,1,0:T(8,128)S(1)} %get-tuple-element.60.refs_0_.refs_2_), channel_id=1, source_target_pairs={{0,8},{8,0},{16,24},{24,16},{1,9},{9,1},{17,25},{25,17},{2,10},{10... | collective-permute-start | bytes 98312 | tf_op jit(solution)/shard_map/ppermute | solution.py:235
  70.2 5.8 %collective-permute-start.18 = (f32[8,8,128]{2,1,0:T(8,128)S(1)}, f32[8,8,128]{2,1,0:T(8,128)S(1)}, u32[]{:S(2)}, u32[]{:S(2)}) collective-permute-start(f32[8,8,128]{2,1,0:T(8,128)S(1)} %get-tuple-element.60.refs_0_.refs_2_), channel_id=1, source_target_pairs={{0,16},{8,24},{16,0},{24,8},{1,17},{9,25},{17,1},{25,9},{2,18},{10... | collective-permute-start | bytes 98312 | tf_op jit(solution)/shard_map/ppermute | solution.py:235
  74.1 6.1 %collective-permute-start.19 = (f32[8,8,128]{2,1,0:T(8,128)S(1)}, f32[8,8,128]{2,1,0:T(8,128)S(1)}, u32[]{:S(2)}, u32[]{:S(2)}) collective-permute-start(f32[8,8,128]{2,1,0:T(8,128)S(1)} %get-tuple-element.60.refs_0_.refs_2_), channel_id=1, source_target_pairs={{0,24},{8,16},{16,8},{24,0},{1,25},{9,17},{17,9},{25,1},{2,26},{10... | collective-permute-start | bytes 98312 | tf_op jit(solution)/shard_map/ppermute | solution.py:235
  80.2 13.4 %collective-permute-start.23 = (f32[32,8,128]{2,1,0:T(8,128)S(1)}, f32[32,8,128]{2,1,0:T(8,128)S(1)}, u32[]{:S(2)}, u32[]{:S(2)}) collective-permute-start(f32[32,8,128]{2,1,0:T(8,128)S(1)} %join_group.2.refs_0_.refs_2_), channel_id=1, source_target_pairs={{0,2},{1,3},{2,0},{3,1},{4,6},{5,7},{6,4},{7,5},{8,10},{9,11},{10,... | collective-permute-start | bytes 393224 | tf_op jit(solution)/shard_map/ppermute | solution.py:235
  81.7 11.9 %collective-permute-start.24 = (f32[32,8,128]{2,1,0:T(8,128)S(1)}, f32[32,8,128]{2,1,0:T(8,128)S(1)}, u32[]{:S(2)}, u32[]{:S(2)}) collective-permute-start(f32[32,8,128]{2,1,0:T(8,128)S(1)} %join_group.2.refs_0_.refs_2_), channel_id=1, source_target_pairs={{0,4},{1,5},{2,6},{3,7},{4,0},{5,1},{6,2},{7,3},{8,12},{9,13},{10,... | collective-permute-start | bytes 393224 | tf_op jit(solution)/shard_map/ppermute | solution.py:235
  83.3 10.4 %collective-permute-start.25 = (f32[32,8,128]{2,1,0:T(8,128)S(1)}, f32[32,8,128]{2,1,0:T(8,128)S(1)}, u32[]{:S(2)}, u32[]{:S(2)}) collective-permute-start(f32[32,8,128]{2,1,0:T(8,128)S(1)} %join_group.2.refs_0_.refs_2_), channel_id=1, source_target_pairs={{0,6},{1,7},{2,4},{3,5},{4,2},{5,3},{6,0},{7,1},{8,14},{9,15},{10,... | collective-permute-start | bytes 393224 | tf_op jit(solution)/shard_map/ppermute | solution.py:235
  83.7 4.8 %collective-permute-start.21 = (f32[8,8,128]{2,1,0:T(8,128)S(1)}, f32[8,8,128]{2,1,0:T(8,128)S(1)}, u32[]{:S(2)}, u32[]{:S(2)}) collective-permute-start(f32[8,8,128]{2,1,0:T(8,128)S(1)} %get-tuple-element.67), channel_id=1, source_target_pairs={{0,16},{8,24},{16,0},{24,8},{1,17},{9,25},{17,1},{25,9},{2,18},{10... | collective-permute-start | bytes 98312 | tf_op jit(solution)/shard_map/ppermute | solution.py:235
  87.7 5.7 %collective-permute-start.22 = (f32[8,8,128]{2,1,0:T(8,128)S(1)}, f32[8,8,128]{2,1,0:T(8,128)S(1)}, u32[]{:S(2)}, u32[]{:S(2)}) collective-permute-start(f32[8,8,128]{2,1,0:T(8,128)S(1)} %get-tuple-element.68), channel_id=1, source_target_pairs={{0,24},{8,16},{16,8},{24,0},{1,25},{9,17},{17,9},{25,1},{2,26},{10... | collective-permute-start | bytes 98312 | tf_op jit(solution)/shard_map/ppermute | solution.py:235
  93.7 21.3 %collective-permute-start.26 = (f32[128,8,128]{2,1,0:T(8,128)S(1)}, f32[128,8,128]{2,1,0:T(8,128)S(1)}, u32[]{:S(2)}, u32[]{:S(2)}) collective-permute-start(f32[128,8,128]{2,1,0:T(8,128)S(1)} %join_plane.2.refs_6_), channel_id=1, source_target_pairs={{0,1},{1,0},{2,3},{3,2},{4,5},{5,4},{6,7},{7,6},{8,9},{9,8},{10,11... | collective-permute-start | bytes 1572872 | tf_op jit(solution)/shard_map/ppermute | solution.py:235
  93.8 4.5 %collective-permute-start.27 = (f32[8,8,128]{2,1,0:T(8,128)S(1)}, f32[8,8,128]{2,1,0:T(8,128)S(1)}, u32[]{:S(2)}, u32[]{:S(2)}) collective-permute-start(f32[8,8,128]{2,1,0:T(8,128)S(1)} %get-tuple-element.71.refs_0_.refs_1_), channel_id=1, source_target_pairs={{0,8},{8,0},{16,24},{24,16},{1,9},{9,1},{17,25},{25,17},{2,10},{10... | collective-permute-start | bytes 98312 | tf_op jit(solution)/shard_map/ppermute | solution.py:235
  93.9 5.0 %collective-permute-start.28 = (f32[8,8,128]{2,1,0:T(8,128)S(1)}, f32[8,8,128]{2,1,0:T(8,128)S(1)}, u32[]{:S(2)}, u32[]{:S(2)}) collective-permute-start(f32[8,8,128]{2,1,0:T(8,128)S(1)} %get-tuple-element.71.refs_0_.refs_1_), channel_id=1, source_target_pairs={{0,16},{8,24},{16,0},{24,8},{1,17},{9,25},{17,1},{25,9},{2,18},{10... | collective-permute-start | bytes 98312 | tf_op jit(solution)/shard_map/ppermute | solution.py:235
  94.9 5.7 %collective-permute-start.29 = (f32[8,8,128]{2,1,0:T(8,128)S(1)}, f32[8,8,128]{2,1,0:T(8,128)S(1)}, u32[]{:S(2)}, u32[]{:S(2)}) collective-permute-start(f32[8,8,128]{2,1,0:T(8,128)S(1)} %get-tuple-element.71.refs_0_.refs_1_), channel_id=1, source_target_pairs={{0,24},{8,16},{16,8},{24,0},{1,25},{9,17},{17,9},{25,1},{2,26},{10... | collective-permute-start | bytes 98312 | tf_op jit(solution)/shard_map/ppermute | solution.py:235
  100.7 25.2 %collective-permute-start.30 = (f32[32,8,128]{2,1,0:T(8,128)S(1)}, f32[32,8,128]{2,1,0:T(8,128)S(1)}, u32[]{:S(2)}, u32[]{:S(2)}) collective-permute-start(f32[32,8,128]{2,1,0:T(8,128)S(1)} %join_group.3.refs_1_.refs_2_), channel_id=1, source_target_pairs={{0,2},{1,3},{2,0},{3,1},{4,6},{5,7},{6,4},{7,5},{8,10},{9,11},{10,... | collective-permute-start | bytes 393224 | tf_op jit(solution)/shard_map/ppermute | solution.py:235
  102.2 23.7 %collective-permute-start.31 = (f32[32,8,128]{2,1,0:T(8,128)S(1)}, f32[32,8,128]{2,1,0:T(8,128)S(1)}, u32[]{:S(2)}, u32[]{:S(2)}) collective-permute-start(f32[32,8,128]{2,1,0:T(8,128)S(1)} %join_group.3.refs_1_.refs_2_), channel_id=1, source_target_pairs={{0,4},{1,5},{2,6},{3,7},{4,0},{5,1},{6,2},{7,3},{8,12},{9,13},{10,... | collective-permute-start | bytes 393224 | tf_op jit(solution)/shard_map/ppermute | solution.py:235
  103.7 22.1 %collective-permute-start.32 = (f32[32,8,128]{2,1,0:T(8,128)S(1)}, f32[32,8,128]{2,1,0:T(8,128)S(1)}, u32[]{:S(2)}, u32[]{:S(2)}) collective-permute-start(f32[32,8,128]{2,1,0:T(8,128)S(1)} %join_group.3.refs_1_.refs_2_), channel_id=1, source_target_pairs={{0,6},{1,7},{2,4},{3,5},{4,2},{5,3},{6,0},{7,1},{8,14},{9,15},{10,... | collective-permute-start | bytes 393224 | tf_op jit(solution)/shard_map/ppermute | solution.py:235
  125.9 10.9 %collective-permute-start.33 = (f32[128,8,128]{2,1,0:T(8,128)S(1)}, f32[128,8,128]{2,1,0:T(8,128)S(1)}, u32[]{:S(2)}, u32[]{:S(2)}) collective-permute-start(f32[128,8,128]{2,1,0:T(8,128)S(1)} %join_plane.3.refs_5_), channel_id=1, source_target_pairs={{0,1},{1,0},{2,3},{3,2},{4,5},{5,4},{6,7},{7,6},{8,9},{9,8},{10,11... | collective-permute-start | bytes 1572872 | tf_op jit(solution)/shard_map/ppermute | solution.py:235
  (2 other events, 8.3 us)

commit v3 on v0

v3 whole, which is shorter than its diff:
```python
import functools

import jax
import jax.numpy as jnp
from jax import lax
from jax.experimental import pallas as pl
from jax.experimental.pallas import tpu as pltpu
from jax.sharding import PartitionSpec as P

F32 = jnp.float32
BF16 = jnp.bfloat16
LANES = 128
MIB = 1 << 20


def split3(x):
    hi = x.astype(BF16).astype(F32)
    rest = x - hi
    mid = rest.astype(BF16).astype(F32)
    low = (rest - mid).astype(BF16).astype(F32)
    return hi, mid, low


def tree_sum(terms):
    terms = list(terms)
    while len(terms) > 1:
        terms = [terms[i] + terms[i + 1] for i in range(0, len(terms), 2)]
    return terms[0]


def left_kernel(g_hbm, e_hbm, q_hbm, both_out, p_out, q_in, sems, *, first):
    count, height, _ = both_out.shape
    rows = height // 2
    rank = q_in.shape[1]

    def fetch(i):
        return (
            pltpu.make_async_copy(q_hbm.at[first + i], q_in.at[i], sems.at[0, i]),
            pltpu.make_async_copy(g_hbm.at[first + i], both_out.at[i, pl.ds(0, rows)], sems.at[1, i]),
            pltpu.make_async_copy(e_hbm.at[first + i], both_out.at[i, pl.ds(rows, rows)], sems.at[2, i]),
        )

    for i in range(count):
        for copy in fetch(i):
            copy.start()

    @pl.loop(0, count)
    def _(i):
        for copy in fetch(i):
            copy.wait()
        basis = jnp.concatenate(split3(q_in[i]), axis=0).astype(BF16)
        part = lax.dot_general(both_out[i], basis, (((1,), (1,)), ((), ())), preferred_element_type=F32)
        part = (part[:rows] + part[rows:]).T
        p_out[i] = part[:rank] + (part[rank : 2 * rank] + part[2 * rank :])


def add_kernel(a_ref, b_ref, out):
    out[...] = a_ref[...] + b_ref[...]


def right_kernel(at_ref, both_ref, *refs):
    p_refs, (sum_out, keep_out, send_out, left) = refs[:-4], refs[-4:]
    count, rank, _ = sum_out.shape
    width = both_ref.shape[2]
    p_sum = tree_sum([r[...] for r in p_refs])
    sum_out[...] = p_sum
    lane = lax.broadcasted_iota(jnp.int32, (rank, LANES), 1)
    gram = jnp.zeros((rank, LANES), F32)
    for m in range(count):
        one = p_sum[m]
        for j in range(rank):
            column = jnp.sum(one * one[j : j + 1], axis=1, keepdims=True)
            gram = jnp.where(lane == j * count + m, column, gram)
        terms = jnp.concatenate(split3(one), axis=0)
        left[m] = jnp.concatenate([terms, terms], axis=1).astype(BF16)
    core = at_ref[0]
    half = keep_out.shape[0] - 1
    step = min(width, 2048)
    per = width // step
    tiles = step // LANES
    for out, mine in ((send_out, 1 - core), (keep_out, core)):
        out[half] = gram

        @pl.loop(0, count // 2 * per)
        def _(at):
            m = mine * (count // 2) + at // per
            start = pl.multiple_of(lax.rem(at, per) * step, step)
            part = jnp.dot(left[m], both_ref[m, :, pl.ds(start, step)], preferred_element_type=F32)
            part = part[:rank] + (part[rank : 2 * rank] + part[2 * rank :])
            for t in range(tiles):
                out[at * tiles + t] = part[:, t * LANES : (t + 1) * LANES]


def fold_kernel(at_ref, a_ref, b_ref, keep_out, send_out, *last_out):
    each = a_ref.shape[0] // 2
    for out, mine in ((send_out, 1 - at_ref[0]), (keep_out, at_ref[0])):
        here = pl.ds(pl.multiple_of(mine * each, each), each)
        out[pl.ds(0, each)] = a_ref[here] + b_ref[here]
    if a_ref.shape[0] % 2:
        last = a_ref[2 * each] + b_ref[2 * each]
        if last_out:
            last_out[0][...] = last
        else:
            keep_out[each] = last
            send_out[each] = last


def join_kernel(at_ref, mine_ref, other_ref, out):
    each = mine_ref.shape[0]
    out[pl.ds(pl.multiple_of(at_ref[0] * each, each), each)] = mine_ref[...]
    out[pl.ds(pl.multiple_of((1 - at_ref[0]) * each, each), each)] = other_ref[...]


def invert(gram, matrices, rank):
    row = lax.broadcasted_iota(jnp.int32, (rank, LANES), 0)
    lane = lax.broadcasted_iota(jnp.int32, (rank, LANES), 1)
    used = lane < matrices
    unit = [jnp.where(row == j, 1.0, 0.0).astype(F32) for j in range(rank)]
    cols = [
        jnp.where(used, gram if j == 0 else pltpu.roll(gram, LANES - j * matrices, 1), unit[j]) for j in range(rank)
    ]
    inverse = list(unit)
    scale = jnp.ones((rank, LANES), F32)
    for k in range(rank):
        pivot = jnp.broadcast_to(cols[k][k : k + 1], (rank, LANES))
        scale = jnp.where(row == k, 1.0 / jnp.sqrt(pivot), scale)
        factor = jnp.where(row > k, cols[k] / pivot, 0.0)
        for j in range(k + 1, rank):
            cols[j] = cols[j] - factor * cols[j][k : k + 1]
        for j in range(k + 1):
            inverse[j] = inverse[j] - factor * inverse[j][k : k + 1]
    return [scale * c for c in inverse]


def piece_kernel(at_ref, gram_ref, a_ref, b_ref, q_out, inv_out, *, per, groups, matrices):
    rank = gram_ref.shape[0]
    inverse = invert(gram_ref[...], matrices, rank)
    for j in range(rank):
        inv_out[j] = inverse[j]
    m = at_ref[0] // per
    lane = lax.broadcasted_iota(jnp.int32, (rank, LANES), 1)
    picked = [
        jnp.broadcast_to(jnp.sum(jnp.where(lane == m, c, 0.0), axis=1, keepdims=True), (rank, LANES)) / groups
        for c in inverse
    ]
    for t in range(q_out.shape[0]):
        total = a_ref[t] + b_ref[t]
        q_out[t] = sum(picked[j] * total[j : j + 1] for j in range(rank))


def out_kernel(at_ref, both_ref, sum_ref, inv_ref, q_ref, *refs, first, flip):
    err_hbm, approx_hbm, q_hbm, token, q_buf, err_buf, approx_buf, left, sems, q_sems = refs[-10:]
    count, rank, rows = sum_ref.shape
    width = both_ref.shape[2]
    slots, _, step = err_buf.shape
    tiles = step // LANES
    per = width // step
    total = count // 2 * per
    base = jnp.bitwise_xor(at_ref[0], flip) * (count // 2)
    token[...] = inv_ref[0]
    lane = lax.broadcasted_iota(jnp.int32, (rank, LANES), 1)

    def results(at):
        slot = lax.rem(at, slots)
        start = pl.multiple_of(lax.rem(at, per) * step, step)
        m = first + base + at // per
        return (
            pltpu.make_async_copy(approx_buf.at[slot], approx_hbm.at[m, :, pl.ds(start, step)], sems.at[0, slot]),
            pltpu.make_async_copy(err_buf.at[slot], err_hbm.at[m, :, pl.ds(start, step)], sems.at[1, slot]),
        )

    def q_result(i):
        return pltpu.make_async_copy(q_buf.at[i], q_hbm.at[first + base + i], q_sems.at[i])

    @pl.loop(0, total)
    def _(at):
        i = at // per
        m = base + i
        slot = lax.rem(at, slots)
        start = pl.multiple_of(lax.rem(at, per) * step, step)

        @pl.when(lax.rem(at, per) == 0)
        def _():
            one = sum_ref[m]
            orth = jnp.zeros((rank, rows), F32)
            for j in range(rank):
                weight = jnp.sum(jnp.where(lane == m, inv_ref[j], 0.0), axis=1, keepdims=True)
                orth = orth + weight * one[j : j + 1]
            hi = orth.astype(BF16).astype(F32)
            low = (orth - hi).astype(BF16).astype(F32)
            left[...] = jnp.concatenate([hi, low, hi], axis=0).T.astype(BF16)

        @pl.when(at >= slots)
        def _():
            for copy in results(at - slots):
                copy.wait()

        half = step // 2
        for k in range(2):
            here = pl.ds(start + k * half, half)
            right = jnp.concatenate([q_ref[at * tiles + k * (tiles // 2) + t] for t in range(tiles // 2)], axis=1)
            q_buf[i, :, here] = right
            hi = right.astype(BF16).astype(F32)
            low = (right - hi).astype(BF16).astype(F32)
            terms = jnp.concatenate([hi, hi, low], axis=0).astype(BF16)
            approx = jnp.dot(left[...], terms, preferred_element_type=F32)
            there = slice(k * half, (k + 1) * half)
            approx_buf[slot, :, there] = approx
            merged = both_ref[m, :rows, here].astype(F32) + both_ref[m, rows:, here].astype(F32)
            err_buf[slot, :, there] = (merged - approx).astype(BF16)
        for copy in results(at):
            copy.start()

        @pl.when(lax.rem(at, per) == per - 1)
        def _():
            q_result(i).start()

    @pl.loop(max(0, total - slots), total)
    def _(at):
        for copy in results(at):
            copy.wait()

    for i in range(count // 2):
        q_result(i).wait()


VMEM = pl.BlockSpec(memory_space=pltpu.VMEM)
HBM = pl.BlockSpec(memory_space=pltpu.HBM)
SMEM = pl.BlockSpec(memory_space=pltpu.SMEM)
ANY = pl.BlockSpec(memory_space=pl.ANY)
CHUNKS = 2
SLOTS = 6
OUT_STEP = 2048


def limit(mib):
    return pltpu.CompilerParams(vmem_limit_bytes=mib * MIB)


def cost(moved):
    return pl.CostEstimate(flops=0, bytes_accessed=moved, transcendentals=0)


def ordered(kernel, count):
    def call(*refs):
        kernel(*refs[count:])

    return call


def on_device(sizes, grad, error, q_prev):
    groups, shards = sizes
    _, layers, pair, rows, width = grad.shape
    matrices = layers * pair
    rank = q_prev.shape[2]
    pieces = groups * shards
    whole = (matrices, rows, width)
    count = matrices // CHUNKS
    half = count // 2 * width // LANES

    def powers(size):
        return [1 << k for k in range(size.bit_length() - 1)]

    chips = [("shard", k) for k in powers(shards) if k > 1]
    lines = [("dp", k) for k in powers(groups)]
    orders = [[("shard", 1)] + (chips[::-1] if c % 2 else chips) + lines for c in range(CHUNKS)]

    def member(name, step):
        return lax.rem(lax.axis_index(name) // step, 2)

    def place(order):
        at = jnp.int32(0)
        for name, step in order:
            at = at * 2 + member(name, step)
        return at

    sides = {line: member(*line).reshape(1) for line in orders[0]}
    places = [place(order).reshape(1) for order in orders]
    core = sides["shard", 1]

    grads, errors, basis = [
        pltpu.with_memory_space_constraint(x, pltpu.HBM)
        for x in (grad.reshape(whole), error.reshape(whole), q_prev.reshape(matrices, rank, width))
    ]

    def tiled(*shape):
        return jax.ShapeDtypeStruct(shape + (rank, LANES), F32)

    def swap(x, name, step):
        return lax.ppermute(x, name, [(i, i ^ step) for i in range(sizes[0] if name == "dp" else sizes[1])])

    latest = list(sides.values()) + places

    def call(kernel, out_shape, at, *args, name, mib=12, moved=0, scratch=(), spaces=None, out_spaces=None, aliases=None):
        after = list(latest)
        ahead = len(after) + (at is not None)
        outs = pl.pallas_call(
            ordered(kernel, len(after)),
            out_shape=out_shape,
            in_specs=[ANY] * len(after) + [SMEM] * (at is not None) + list(spaces or [VMEM] * len(args)),
            out_specs=out_spaces or jax.tree.map(lambda _: VMEM, out_shape),
            scratch_shapes=list(scratch),
            input_output_aliases={ahead + k: v for k, v in (aliases or {}).items()},
            compiler_params=limit(mib),
            cost_estimate=cost(moved),
            name=name,
        )(*after, *([at] if at is not None else []), *args)
        last = outs[-1] if isinstance(outs, (tuple, list)) else outs
        latest[:] = [last]
        return outs

    p_shape = jax.ShapeDtypeStruct((count, rank, rows), F32)
    boths, owns = [], []
    for c in range(CHUNKS):
        both, own = call(
            functools.partial(left_kernel, first=c * count),
            (pltpu.VMEM((count, 2 * rows, width), BF16), p_shape),
            None, grads, errors, basis,
            name="left", mib=12, moved=count * rows * width, spaces=[HBM] * 3,
            scratch=[pltpu.VMEM((count, rank, width), F32), pltpu.SemaphoreType.DMA((3, count))],
        )
        boths.append(pltpu.with_memory_space_constraint(both, pltpu.VMEM))
        owns.append([own, swap(own, *lines[0])])
    for line in lines[1:]:
        for c in range(CHUNKS):
            own = call(add_kernel, p_shape, None, *owns[c], name="add")
            owns[c] = [own, swap(own, *line)]
    sums, kept = [], []
    for c in range(CHUNKS):
        keep, send, p_sum = call(
            lambda at, both, *refs: right_kernel(at, both, *refs[:-4], refs[-2], refs[-4], refs[-3], refs[-1]),
            (tiled(half + 1), tiled(half + 1), p_shape),
            core, boths[c], *owns[c],
            name="right", moved=count * rows * width, scratch=[pltpu.VMEM((count, 3 * rank, 2 * rows), BF16)],
        )
        sums.append(p_sum)
        kept.append((keep, swap(send, *orders[c][0])))

    size = half
    grams = [None] * CHUNKS
    for stage in range(1, len(orders[0])):
        size //= 2
        for c in range(CHUNKS):
            name, step = orders[c][stage]
            with_gram = name == "shard"
            shape = (tiled(size + with_gram),) * 2
            if orders[c][stage - 1][0] == "shard" and not with_gram:
                shape += (tiled(),)
            outs = call(
                fold_kernel, shape, sides[name, step], *kept[c], name="fold"
            )
            if len(outs) == 3:
                grams[c] = outs[2]
            kept[c] = (outs[0], swap(outs[1], name, step))
    ready, inverses = [], []
    for c in range(CHUNKS):
        piece, inverse = call(
            functools.partial(piece_kernel, per=pieces // count, groups=groups, matrices=count),
            (tiled(size), tiled(rank)),
            places[c], grams[c], *kept[c], name="piece",
        )
        inverses.append(inverse)
        ready.append((piece, swap(piece, *orders[c][-1])))

    def join(c, stage):
        mine = call(
            join_kernel, tiled(2 * ready[c][0].shape[0]), sides[orders[c][stage]], *ready[c], name="join",
        )
        ready[c] = (mine, swap(mine, *orders[c][stage - 1]))

    for stage in range(len(orders[0]) - 1, 1, -1):
        for c in range(CHUNKS):
            join(c, stage)
    results = []
    for c in range(CHUNKS):
        join(c, 1)
        for flip in range(2):
            *results, token = call(
                functools.partial(out_kernel, first=c * count, flip=flip),
                (
                    jax.ShapeDtypeStruct(whole, BF16),
                    jax.ShapeDtypeStruct(whole, F32),
                    jax.ShapeDtypeStruct((matrices, rank, width), F32),
                    tiled(),
                ),
                core, boths[c], sums[c], inverses[c], ready[c][flip], *results,
                name="out", moved=count * rows * width,
                spaces=[VMEM] * 4 + [HBM] * len(results), out_spaces=(HBM, HBM, HBM, VMEM),
                aliases={4 + k: k for k in range(len(results))},
                scratch=[
                    pltpu.VMEM((count // 2, rank, width), F32),
                    pltpu.VMEM((SLOTS, rows, OUT_STEP), BF16),
                    pltpu.VMEM((SLOTS, rows, OUT_STEP), F32),
                    pltpu.VMEM((rows, 3 * rank), BF16),
                    pltpu.SemaphoreType.DMA((2, SLOTS)),
                    pltpu.SemaphoreType.DMA((count // 2,)),
                ],
            )
    error_out, approx, q_new = results
    return error_out.reshape(grad.shape), approx.reshape(layers, pair, rows, width), q_new.reshape(q_prev.shape)


def solution(mesh):
    sizes = (mesh.shape["dp"], mesh.shape["shard"])
    in_specs = (P("dp", None, None, "shard", None), P("dp", None, None, "shard", None), P())
    out_specs = (P("dp", None, None, "shard", None), P(None, None, "shard", None), P())
    return jax.shard_map(
        functools.partial(on_device, sizes), mesh=mesh, in_specs=in_specs, out_specs=out_specs, check_vma=False
    )
```

time: 477 us -> 111 us (0.23)
  blocking collectives: 210 us -> 0 us
  waiting for transfers between devices: 131 us -> 25.7 us
  matrix products: 94.1 us -> 0 us
  Pallas kernels: 0 us -> 47.3 us
  starting transfers between devices: 0.04 us -> 36.8 us
  other arithmetic: 26.6 us -> 0 us
  between operations: 14.2 us -> 0.93 us
    psum x17 -> x0, blocking collectives: 210 us -> none  [the longest x8 94.6 us: on_device(): norm = lax.psum(jnp.sum(column * column, axis=1), 'shard')]
    psum x1 -> x0, waiting for transfers between devices: 131 us -> none  [on_device(): total_q = lax.psum(local_q, ('dp', 'shard'))]
    dot_general x19 -> x0, matrix products: 94.1 us -> none  [the longest x1 37.9 us: on_device(): approx = jnp.einsum('mrk,mkd->mrd', p_orth, q_new, precision=highest)]
    pallas_call x0 -> x28, Pallas kernels: none -> 47.3 us  [call(): pl.pallas_call(ordered(kernel, len(after)), out_shape=out_shape, in_specs...]
    ppermute x0 -> x24, starting transfers between devices: none -> 36.8 us  [swap(): lax.ppermute(x, name, [(i, i ^ step) for i in range(sizes[0] if name == '...]
    ppermute x0 -> x24, waiting for transfers between devices: none -> 25.7 us  [swap(): lax.ppermute(x, name, [(i, i ^ step) for i in range(sizes[0] if name == '...]
    add x1 -> x0, other arithmetic: 23.5 us -> none  [on_device(): grad.astype(jnp.float32) + error.astype(jnp.float32)]
  transfers between devices with their start and end apart: 1 -> 24, of which waited for: 1 -> 11; matrix products, arithmetic and copies ran while one was open for 0% -> 0% of each run, Pallas kernels for 0% -> 26%
where the time goes in v3:
time: 111 us
  Pallas kernels  47.3 us (43%)
  starting transfers between devices  36.8 us (33%)
  waiting for transfers between devices  25.7 us (23%)
    pallas_call x28, Pallas kernels, call(): pl.pallas_call(ordered(kernel, len(after)), out_shape=out_shape, in_specs...  47.3 us
    ppermute x24, starting transfers between devices, swap(): lax.ppermute(x, name, [(i, i ^ step) for i in range(sizes[0] if name == '...  36.8 us
    ppermute x24, waiting for transfers between devices, swap(): lax.ppermute(x, name, [(i, i ^ step) for i in range(sizes[0] if name == '...  25.7 us
  transfers between devices with their start and end apart: 24, of which 11 were waited for; matrix products, arithmetic and copies ran while one was open for 0% of the time, Pallas kernels for 26%

profile of v3, /device:TPU:0, one launch (start us, length us, event | category | flops | bytes accessed | tf_op | source)
XLA Modules:
  0.0 110.7 jit_solution(4893557205109298064)
XLA Ops:
  0.7 7.5 %left.2 = (bf16[4,256,8192]{2,1,0:T(8,128)(2,1)S(1)}, f32[4,8,128]{2,1,0:T(8,128)S(1)}) custom-call(s32[1]{0:T(128)} %bitcast.refs_0_.refs_1_, s32[1]{0:T(128)} %bitcast.1.refs_1_, s32[1]{0:T(128)} %bitcast.2.refs_2_.refs_1_, s32[1]{0:T(128)} %bitcast.3.refs_3_.refs_1_, s32[1]{0:T(128)} %bitcast.4.refs_4_.refs_1_, s32[1]{0:T(128)} %bitcast.5.refs_5_.refs_1_, ...), custom_call_target="tpu_custom_call" | custom-call | bytes 4194304 | tf_op jit(solution)/shard_map/left/pallas_call | solution.py:297
  8.2 3.1 %collective-permute-start = (f32[4,8,128]{2,1,0:T(8,128)S(1)}, f32[4,8,128]{2,1,0:T(8,128)S(1)}, u32[]{:S(2)}, u32[]{:S(2)}) collective-permute-start(f32[4,8,128]{2,1,0:T(8,128)S(1)} %get-tuple-element.50.refs_0_.refs_1_), channel_id=1, source_target_pairs={{0,8},{8,0},{16,24},{24,16},{1,9},{9,1},{17,25},{25,17},{2,10},{10... | collective-permute-start | bytes 49160 | tf_op jit(solution)/shard_map/ppermute | solution.py:290
  11.3 7.5 %left.3 = (bf16[4,256,8192]{2,1,0:T(8,128)(2,1)S(1)}, f32[4,8,128]{2,1,0:T(8,128)S(1)}) custom-call(f32[4,8,128]{2,1,0:T(8,128)S(1)} %get-tuple-element.50.refs_0_.refs_1_, bf16[8,128,8192]{2,1,0:T(8,128)(2,1)} %bitcast.16, bf16[8,128,8192]{2,1,0:T(8,128)(2,1)} %bitcast.18, f32[8,8,8192]{2,1,0:T(8,128)} %bitcast.21), custom_call_target="tpu_custom_call" | custom-call | bytes 4194304 | tf_op jit(solution)/shard_map/left/pallas_call | solution.py:297
  19.0 3.1 %collective-permute-start.2 = (f32[4,8,128]{2,1,0:T(8,128)S(1)}, f32[4,8,128]{2,1,0:T(8,128)S(1)}, u32[]{:S(2)}, u32[]{:S(2)}) collective-permute-start(f32[4,8,128]{2,1,0:T(8,128)S(1)} %add.39.refs_0_.refs_3_), channel_id=1, source_target_pairs={{0,16},{8,24},{16,0},{24,8},{1,17},{9,25},{17,1},{25,9},{2,18},{10... | collective-permute-start | bytes 49160 | tf_op jit(solution)/shard_map/ppermute | solution.py:290
  23.8 4.8 %right.2 = (f32[129,8,128]{2,1,0:T(8,128)S(1)}, f32[129,8,128]{2,1,0:T(8,128)S(1)}, f32[4,8,128]{2,1,0:T(8,128)S(1)}) custom-call(f32[4,8,128]{2,1,0:T(8,128)S(1)} %add.40.refs_0_.refs_3_, s32[1]{0:T(128)} %bitcast.refs_0_.refs_1_, bf16[4,256,8192]{2,1,0:T(8,128)(2,1)S(1)} %get-tuple-element.52.refs_2_, f32[4,8,128]{2,1,0:T(8,128)S(1)} %add.39.refs_0_.refs_3_, ...), custom_call_target="tpu_custom_call" | custom-call | bytes 4194304 | tf_op jit(solution)/shard_map/right/pallas_call | solution.py:297
  28.6 3.0 %collective-permute-start.3 = (f32[4,8,128]{2,1,0:T(8,128)S(1)}, f32[4,8,128]{2,1,0:T(8,128)S(1)}, u32[]{:S(2)}, u32[]{:S(2)}) collective-permute-start(f32[4,8,128]{2,1,0:T(8,128)S(1)} %add.40.refs_0_.refs_3_), channel_id=1, source_target_pairs={{0,16},{8,24},{16,0},{24,8},{1,17},{9,25},{17,1},{25,9},{2,18},{10... | collective-permute-start | bytes 49160 | tf_op jit(solution)/shard_map/ppermute | solution.py:290
  31.6 1.7 %collective-permute-done.3.refs_4_ = f32[4,8,128]{2,1,0:T(8,128)S(1)} collective-permute-done((f32[4,8,128]{2,1,0:T(8,128)S(1)}, f32[4,8,128]{2,1,0:T(8,128)S(1)}, u32[]{:S(2)}, u32[]{:S(2)}) %collective-permute-start.3) | collective-permute-done | bytes 16416 | tf_op jit(solution)/shard_map/ppermute | solution.py:290
  33.3 4.8 %right.3 = (f32[129,8,128]{2,1,0:T(8,128)S(1)}, f32[129,8,128]{2,1,0:T(8,128)S(1)}, f32[4,8,128]{2,1,0:T(8,128)S(1)}) custom-call(f32[4,8,128]{2,1,0:T(8,128)S(1)} %get-tuple-element.53.refs_0_.refs_3_, s32[1]{0:T(128)} %bitcast.refs_0_.refs_1_, bf16[4,256,8192]{2,1,0:T(8,128)(2,1)S(1)} %get-tuple-element.54.refs_2_, f32[4,8,128]{2,1,0:T(8,128)S(1)} %add.40.refs_0_.refs_3_, ...), custom_call_target="tpu_custom_call" | custom-call | bytes 4194304 | tf_op jit(solution)/shard_map/right/pallas_call | solution.py:297
  38.2 1.9 %collective-permute-start.6 = (f32[65,8,128]{2,1,0:T(8,128)S(1)}, f32[65,8,128]{2,1,0:T(8,128)S(1)}, u32[]{:S(2)}, u32[]{:S(2)}) collective-permute-start(f32[65,8,128]{2,1,0:T(8,128)S(1)} %get-tuple-element.58.refs_0_), channel_id=1, source_target_pairs={{0,2},{1,3},{2,0},{3,1},{4,6},{5,7},{6,4},{7,5},{8,10},{9,11},{10,... | collective-permute-start | bytes 798728 | tf_op jit(solution)/shard_map/ppermute | solution.py:290
  40.2 1.8 %collective-permute-start.7 = (f32[65,8,128]{2,1,0:T(8,128)S(1)}, f32[65,8,128]{2,1,0:T(8,128)S(1)}, u32[]{:S(2)}, u32[]{:S(2)}) collective-permute-start(f32[65,8,128]{2,1,0:T(8,128)S(1)} %get-tuple-element.61.refs_0_), channel_id=1, source_target_pairs={{0,4},{1,5},{2,6},{3,7},{4,0},{5,1},{6,2},{7,3},{8,12},{9,13},{10,... | collective-permute-start | bytes 798728 | tf_op jit(solution)/shard_map/ppermute | solution.py:290
  42.1 5.1 %collective-permute-done.6.refs_3_ = f32[65,8,128]{2,1,0:T(8,128)S(1)} collective-permute-done((f32[65,8,128]{2,1,0:T(8,128)S(1)}, f32[65,8,128]{2,1,0:T(8,128)S(1)}, u32[]{:S(2)}, u32[]{:S(2)}) %collective-permute-start.6) | collective-permute-done | bytes 266272 | tf_op jit(solution)/shard_map/ppermute | solution.py:290
  47.2 1.8 %collective-permute-start.8 = (f32[33,8,128]{2,1,0:T(8,128)S(1)}, f32[33,8,128]{2,1,0:T(8,128)S(1)}, u32[]{:S(2)}, u32[]{:S(2)}) collective-permute-start(f32[33,8,128]{2,1,0:T(8,128)S(1)} %get-tuple-element.63.refs_0_), channel_id=1, source_target_pairs={{0,4},{1,5},{2,6},{3,7},{4,0},{5,1},{6,2},{7,3},{8,12},{9,13},{10,... | collective-permute-start | bytes 405512 | tf_op jit(solution)/shard_map/ppermute | solution.py:290
  49.1 1.6 %collective-permute-start.9 = (f32[33,8,128]{2,1,0:T(8,128)S(1)}, f32[33,8,128]{2,1,0:T(8,128)S(1)}, u32[]{:S(2)}, u32[]{:S(2)}) collective-permute-start(f32[33,8,128]{2,1,0:T(8,128)S(1)} %get-tuple-element.65.refs_0_), channel_id=1, source_target_pairs={{0,2},{1,3},{2,0},{3,1},{4,6},{5,7},{6,4},{7,5},{8,10},{9,11},{10,... | collective-permute-start | bytes 405512 | tf_op jit(solution)/shard_map/ppermute | solution.py:290
  50.6 1.9 %collective-permute-done.8.refs_3_ = f32[33,8,128]{2,1,0:T(8,128)S(1)} collective-permute-done((f32[33,8,128]{2,1,0:T(8,128)S(1)}, f32[33,8,128]{2,1,0:T(8,128)S(1)}, u32[]{:S(2)}, u32[]{:S(2)}) %collective-permute-start.8) | collective-permute-done | bytes 135200 | tf_op jit(solution)/shard_map/ppermute | solution.py:290
  52.6 1.8 %collective-permute-start.10 = (f32[16,8,128]{2,1,0:T(8,128)S(1)}, f32[16,8,128]{2,1,0:T(8,128)S(1)}, u32[]{:S(2)}, u32[]{:S(2)}) collective-permute-start(f32[16,8,128]{2,1,0:T(8,128)S(1)} %get-tuple-element.71), channel_id=1, source_target_pairs={{0,8},{8,0},{16,24},{24,16},{1,9},{9,1},{17,25},{25,17},{2,10},{10... | collective-permute-start | bytes 196616 | tf_op jit(solution)/shard_map/ppermute | solution.py:290
  54.4 1.4 %collective-permute-start.11 = (f32[16,8,128]{2,1,0:T(8,128)S(1)}, f32[16,8,128]{2,1,0:T(8,128)S(1)}, u32[]{:S(2)}, u32[]{:S(2)}) collective-permute-start(f32[16,8,128]{2,1,0:T(8,128)S(1)} %get-tuple-element.74), channel_id=1, source_target_pairs={{0,8},{8,0},{16,24},{24,16},{1,9},{9,1},{17,25},{25,17},{2,10},{10... | collective-permute-start | bytes 196616 | tf_op jit(solution)/shard_map/ppermute | solution.py:290
  57.0 2.7 %collective-permute-start.12 = (f32[8,8,128]{2,1,0:T(8,128)S(1)}, f32[8,8,128]{2,1,0:T(8,128)S(1)}, u32[]{:S(2)}, u32[]{:S(2)}) collective-permute-start(f32[8,8,128]{2,1,0:T(8,128)S(1)} %get-tuple-element.72.refs_0_), channel_id=1, source_target_pairs={{0,16},{8,24},{16,0},{24,8},{1,17},{9,25},{17,1},{25,9},{2,18},{10... | collective-permute-start | bytes 98312 | tf_op jit(solution)/shard_map/ppermute | solution.py:290
  59.7 1.7 %collective-permute-start.13 = (f32[8,8,128]{2,1,0:T(8,128)S(1)}, f32[8,8,128]{2,1,0:T(8,128)S(1)}, u32[]{:S(2)}, u32[]{:S(2)}) collective-permute-start(f32[8,8,128]{2,1,0:T(8,128)S(1)} %get-tuple-element.75.refs_0_), channel_id=1, source_target_pairs={{0,16},{8,24},{16,0},{24,8},{1,17},{9,25},{17,1},{25,9},{2,18},{10... | collective-permute-start | bytes 98312 | tf_op jit(solution)/shard_map/ppermute | solution.py:290
  62.5 2.4 %collective-permute-start.14 = (f32[8,8,128]{2,1,0:T(8,128)S(1)}, f32[8,8,128]{2,1,0:T(8,128)S(1)}, u32[]{:S(2)}, u32[]{:S(2)}) collective-permute-start(f32[8,8,128]{2,1,0:T(8,128)S(1)} %get-tuple-element.80.refs_2_), channel_id=1, source_target_pairs={{0,16},{8,24},{16,0},{24,8},{1,17},{9,25},{17,1},{25,9},{2,18},{10... | collective-permute-start | bytes 98312 | tf_op jit(solution)/shard_map/ppermute | solution.py:290
  65.1 2.2 %collective-permute-done.14.refs_3_ = f32[8,8,128]{2,1,0:T(8,128)S(1)} collective-permute-done((f32[8,8,128]{2,1,0:T(8,128)S(1)}, f32[8,8,128]{2,1,0:T(8,128)S(1)}, u32[]{:S(2)}, u32[]{:S(2)}) %collective-permute-start.14) | collective-permute-done | bytes 32800 | tf_op jit(solution)/shard_map/ppermute | solution.py:290
  67.4 1.6 %collective-permute-start.16 = (f32[16,8,128]{2,1,0:T(8,128)S(1)}, f32[16,8,128]{2,1,0:T(8,128)S(1)}, u32[]{:S(2)}, u32[]{:S(2)}) collective-permute-start(f32[16,8,128]{2,1,0:T(8,128)S(1)} %join.8.refs_0_.refs_2_), channel_id=1, source_target_pairs={{0,8},{8,0},{16,24},{24,16},{1,9},{9,1},{17,25},{25,17},{2,10},{10... | collective-permute-start | bytes 196616 | tf_op jit(solution)/shard_map/ppermute | solution.py:290
  68.9 2.8 %collective-permute-start.15 = (f32[8,8,128]{2,1,0:T(8,128)S(1)}, f32[8,8,128]{2,1,0:T(8,128)S(1)}, u32[]{:S(2)}, u32[]{:S(2)}) collective-permute-start(f32[8,8,128]{2,1,0:T(8,128)S(1)} %get-tuple-element.81.refs_2_), channel_id=1, source_target_pairs={{0,16},{8,24},{16,0},{24,8},{1,17},{9,25},{17,1},{25,9},{2,18},{10... | collective-permute-start | bytes 98312 | tf_op jit(solution)/shard_map/ppermute | solution.py:290
  71.7 2.4 %collective-permute-done.15.refs_3_ = f32[8,8,128]{2,1,0:T(8,128)S(1)} collective-permute-done((f32[8,8,128]{2,1,0:T(8,128)S(1)}, f32[8,8,128]{2,1,0:T(8,128)S(1)}, u32[]{:S(2)}, u32[]{:S(2)}) %collective-permute-start.15) | collective-permute-done | bytes 32800 | tf_op jit(solution)/shard_map/ppermute | solution.py:290
  74.1 1.2 %collective-permute-start.18 = (f32[32,8,128]{2,1,0:T(8,128)S(1)}, f32[32,8,128]{2,1,0:T(8,128)S(1)}, u32[]{:S(2)}, u32[]{:S(2)}) collective-permute-start(f32[32,8,128]{2,1,0:T(8,128)S(1)} %join.10.refs_0_.refs_2_), channel_id=1, source_target_pairs={{0,4},{1,5},{2,6},{3,7},{4,0},{5,1},{6,2},{7,3},{8,12},{9,13},{10,... | collective-permute-start | bytes 393224 | tf_op jit(solution)/shard_map/ppermute | solution.py:290
  75.4 1.3 %collective-permute-start.17 = (f32[16,8,128]{2,1,0:T(8,128)S(1)}, f32[16,8,128]{2,1,0:T(8,128)S(1)}, u32[]{:S(2)}, u32[]{:S(2)}) collective-permute-start(f32[16,8,128]{2,1,0:T(8,128)S(1)} %join.9.refs_0_.refs_2_), channel_id=1, source_target_pairs={{0,8},{8,0},{16,24},{24,16},{1,9},{9,1},{17,25},{25,17},{2,10},{10... | collective-permute-start | bytes 196616 | tf_op jit(solution)/shard_map/ppermute | solution.py:290
  76.7 3.0 %collective-permute-done.17.refs_3_ = f32[16,8,128]{2,1,0:T(8,128)S(1)} collective-permute-done((f32[16,8,128]{2,1,0:T(8,128)S(1)}, f32[16,8,128]{2,1,0:T(8,128)S(1)}, u32[]{:S(2)}, u32[]{:S(2)}) %collective-permute-start.17) | collective-permute-done | bytes 65568 | tf_op jit(solution)/shard_map/ppermute | solution.py:290
  79.7 1.6 %collective-permute-start.20 = (f32[64,8,128]{2,1,0:T(8,128)S(1)}, f32[64,8,128]{2,1,0:T(8,128)S(1)}, u32[]{:S(2)}, u32[]{:S(2)}) collective-permute-start(f32[64,8,128]{2,1,0:T(8,128)S(1)} %join.12.refs_0_.refs_2_), channel_id=1, source_target_pairs={{0,2},{1,3},{2,0},{3,1},{4,6},{5,7},{6,4},{7,5},{8,10},{9,11},{10,... | collective-permute-start | bytes 786440 | tf_op jit(solution)/shard_map/ppermute | solution.py:290
  81.8 5.8 %collective-permute-done.19.refs_3_ = f32[32,8,128]{2,1,0:T(8,128)S(1)} collective-permute-done((f32[32,8,128]{2,1,0:T(8,128)S(1)}, f32[32,8,128]{2,1,0:T(8,128)S(1)}, u32[]{:S(2)}, u32[]{:S(2)}) %collective-permute-start.19) | collective-permute-done | bytes 131104 | tf_op jit(solution)/shard_map/ppermute | solution.py:290
  88.6 5.3 %out.4 = (bf16[8,128,8192]{2,1,0:T(8,128)(2,1)}, f32[8,128,8192]{2,1,0:T(8,128)}, f32[8,8,8192]{2,1,0:T(8,128)}, f32[8,128]{1,0:T(8,128)S(1)}) custom-call(f32[128,8,128]{2,1,0:T(8,128)S(1)} %join.14.refs_0_.refs_5_, s32[1]{0:T(128)} %bitcast.refs_0_.refs_1_, bf16[4,256,8192]{2,1,0:T(8,128)(2,1)S(1)} %get-tuple-element.52.refs_2_, ...), custom_call_target="tpu_custom_call" | custom-call | bytes 4194304 | tf_op jit(solution)/shard_map/out/pallas_call | solution.py:297
  93.9 5.3 %out.5 = (bf16[8,128,8192]{2,1,0:T(8,128)(2,1)}, f32[8,128,8192]{2,1,0:T(8,128)}, f32[8,8,8192]{2,1,0:T(8,128)}, f32[8,128]{1,0:T(8,128)S(1)}) custom-call(f32[8,128]{1,0:T(8,128)S(1)} %get-tuple-element.82.refs_0_, s32[1]{0:T(128)} %bitcast.refs_0_.refs_1_, ...), custom_call_target="tpu_custom_call", output_to_operand_aliasing={{0}: (6, {}), {1}: (7, {}), {2}: (8, {})} | custom-call | bytes 4194304 | tf_op jit(solution)/shard_map/out/pallas_call | solution.py:297
  99.5 5.3 %out.6 = (bf16[8,128,8192]{2,1,0:T(8,128)(2,1)}, f32[8,128,8192]{2,1,0:T(8,128)}, f32[8,8,8192]{2,1,0:T(8,128)}, f32[8,128]{1,0:T(8,128)S(1)}) custom-call(f32[128,8,128]{2,1,0:T(8,128)S(1)} %join.15.refs_0_.refs_5_, s32[1]{0:T(128)} %bitcast.refs_0_.refs_1_, ...), custom_call_target="tpu_custom_call", output_to_operand_aliasing={{0}: (6, {}), {1}: (7, {}), {2}: (8, {})} | custom-call | bytes 4194304 | tf_op jit(solution)/shard_map/out/pallas_call | solution.py:297
  104.8 5.9 %out.7 = (bf16[8,128,8192]{2,1,0:T(8,128)(2,1)}, f32[8,128,8192]{2,1,0:T(8,128)}, f32[8,8,8192]{2,1,0:T(8,128)}, f32[8,128]{1,0:T(8,128)}) custom-call(f32[8,128]{1,0:T(8,128)S(1)} %get-tuple-element.90.refs_0_, s32[1]{0:T(128)} %bitcast.refs_0_.refs_1_, ...), custom_call_target="tpu_custom_call", output_to_operand_aliasing={{0}: (6, {}), {1}: (7, {}), {2}: (8, {})} | custom-call | bytes 4194304 | tf_op jit(solution)/shard_map/out/pallas_call | solution.py:297
  (44 shorter events, 6.5 us)
Async XLA Ops:
  8.2 10.7 %collective-permute-start = (f32[4,8,128]{2,1,0:T(8,128)S(1)}, f32[4,8,128]{2,1,0:T(8,128)S(1)}, u32[]{:S(2)}, u32[]{:S(2)}) collective-permute-start(f32[4,8,128]{2,1,0:T(8,128)S(1)} %get-tuple-element.50.refs_0_.refs_1_), channel_id=1, source_target_pairs={{0,8},{8,0},{16,24},{24,16},{1,9},{9,1},{17,25},{25,17},{2,10},{10... | collective-permute-start | bytes 49160 | tf_op jit(solution)/shard_map/ppermute | solution.py:290
  18.9 3.8 %collective-permute-start.1 = (f32[4,8,128]{2,1,0:T(8,128)S(1)}, f32[4,8,128]{2,1,0:T(8,128)S(1)}, u32[]{:S(2)}, u32[]{:S(2)}) collective-permute-start(f32[4,8,128]{2,1,0:T(8,128)S(1)} %get-tuple-element.51.refs_0_.refs_1_), channel_id=1, source_target_pairs={{0,8},{8,0},{16,24},{24,16},{1,9},{9,1},{17,25},{25,17},{2,10},{10... | collective-permute-start | bytes 49160 | tf_op jit(solution)/shard_map/ppermute | solution.py:290
  19.0 4.8 %collective-permute-start.2 = (f32[4,8,128]{2,1,0:T(8,128)S(1)}, f32[4,8,128]{2,1,0:T(8,128)S(1)}, u32[]{:S(2)}, u32[]{:S(2)}) collective-permute-start(f32[4,8,128]{2,1,0:T(8,128)S(1)} %add.39.refs_0_.refs_3_), channel_id=1, source_target_pairs={{0,16},{8,24},{16,0},{24,8},{1,17},{9,25},{17,1},{25,9},{2,18},{10... | collective-permute-start | bytes 49160 | tf_op jit(solution)/shard_map/ppermute | solution.py:290
  28.5 9.6 %collective-permute-start.4 = (f32[129,8,128]{2,1,0:T(8,128)S(1)}, f32[129,8,128]{2,1,0:T(8,128)S(1)}, u32[]{:S(2)}, u32[]{:S(2)}) collective-permute-start(f32[129,8,128]{2,1,0:T(8,128)S(1)} %get-tuple-element.57), channel_id=1, source_target_pairs={{0,1},{1,0},{2,3},{3,2},{4,5},{5,4},{6,7},{7,6},{8,9},{9,8},{10,11... | collective-permute-start | bytes 1585160 | tf_op jit(solution)/shard_map/ppermute | solution.py:290
  28.6 4.7 %collective-permute-start.3 = (f32[4,8,128]{2,1,0:T(8,128)S(1)}, f32[4,8,128]{2,1,0:T(8,128)S(1)}, u32[]{:S(2)}, u32[]{:S(2)}) collective-permute-start(f32[4,8,128]{2,1,0:T(8,128)S(1)} %add.40.refs_0_.refs_3_), channel_id=1, source_target_pairs={{0,16},{8,24},{16,0},{24,8},{1,17},{9,25},{17,1},{25,9},{2,18},{10... | collective-permute-start | bytes 49160 | tf_op jit(solution)/shard_map/ppermute | solution.py:290
  38.1 2.0 %collective-permute-start.5 = (f32[129,8,128]{2,1,0:T(8,128)S(1)}, f32[129,8,128]{2,1,0:T(8,128)S(1)}, u32[]{:S(2)}, u32[]{:S(2)}) collective-permute-start(f32[129,8,128]{2,1,0:T(8,128)S(1)} %get-tuple-element.60), channel_id=1, source_target_pairs={{0,1},{1,0},{2,3},{3,2},{4,5},{5,4},{6,7},{7,6},{8,9},{9,8},{10,11... | collective-permute-start | bytes 1585160 | tf_op jit(solution)/shard_map/ppermute | solution.py:290
  38.2 8.9 %collective-permute-start.6 = (f32[65,8,128]{2,1,0:T(8,128)S(1)}, f32[65,8,128]{2,1,0:T(8,128)S(1)}, u32[]{:S(2)}, u32[]{:S(2)}) collective-permute-start(f32[65,8,128]{2,1,0:T(8,128)S(1)} %get-tuple-element.58.refs_0_), channel_id=1, source_target_pairs={{0,2},{1,3},{2,0},{3,1},{4,6},{5,7},{6,4},{7,5},{8,10},{9,11},{10,... | collective-permute-start | bytes 798728 | tf_op jit(solution)/shard_map/ppermute | solution.py:290
  40.2 8.8 %collective-permute-start.7 = (f32[65,8,128]{2,1,0:T(8,128)S(1)}, f32[65,8,128]{2,1,0:T(8,128)S(1)}, u32[]{:S(2)}, u32[]{:S(2)}) collective-permute-start(f32[65,8,128]{2,1,0:T(8,128)S(1)} %get-tuple-element.61.refs_0_), channel_id=1, source_target_pairs={{0,4},{1,5},{2,6},{3,7},{4,0},{5,1},{6,2},{7,3},{8,12},{9,13},{10,... | collective-permute-start | bytes 798728 | tf_op jit(solution)/shard_map/ppermute | solution.py:290
  47.2 5.3 %collective-permute-start.8 = (f32[33,8,128]{2,1,0:T(8,128)S(1)}, f32[33,8,128]{2,1,0:T(8,128)S(1)}, u32[]{:S(2)}, u32[]{:S(2)}) collective-permute-start(f32[33,8,128]{2,1,0:T(8,128)S(1)} %get-tuple-element.63.refs_0_), channel_id=1, source_target_pairs={{0,4},{1,5},{2,6},{3,7},{4,0},{5,1},{6,2},{7,3},{8,12},{9,13},{10,... | collective-permute-start | bytes 405512 | tf_op jit(solution)/shard_map/ppermute | solution.py:290
  49.1 5.3 %collective-permute-start.9 = (f32[33,8,128]{2,1,0:T(8,128)S(1)}, f32[33,8,128]{2,1,0:T(8,128)S(1)}, u32[]{:S(2)}, u32[]{:S(2)}) collective-permute-start(f32[33,8,128]{2,1,0:T(8,128)S(1)} %get-tuple-element.65.refs_0_), channel_id=1, source_target_pairs={{0,2},{1,3},{2,0},{3,1},{4,6},{5,7},{6,4},{7,5},{8,10},{9,11},{10,... | collective-permute-start | bytes 405512 | tf_op jit(solution)/shard_map/ppermute | solution.py:290
  52.6 4.4 %collective-permute-start.10 = (f32[16,8,128]{2,1,0:T(8,128)S(1)}, f32[16,8,128]{2,1,0:T(8,128)S(1)}, u32[]{:S(2)}, u32[]{:S(2)}) collective-permute-start(f32[16,8,128]{2,1,0:T(8,128)S(1)} %get-tuple-element.71), channel_id=1, source_target_pairs={{0,8},{8,0},{16,24},{24,16},{1,9},{9,1},{17,25},{25,17},{2,10},{10... | collective-permute-start | bytes 196616 | tf_op jit(solution)/shard_map/ppermute | solution.py:290
  54.4 5.3 %collective-permute-start.11 = (f32[16,8,128]{2,1,0:T(8,128)S(1)}, f32[16,8,128]{2,1,0:T(8,128)S(1)}, u32[]{:S(2)}, u32[]{:S(2)}) collective-permute-start(f32[16,8,128]{2,1,0:T(8,128)S(1)} %get-tuple-element.74), channel_id=1, source_target_pairs={{0,8},{8,0},{16,24},{24,16},{1,9},{9,1},{17,25},{25,17},{2,10},{10... | collective-permute-start | bytes 196616 | tf_op jit(solution)/shard_map/ppermute | solution.py:290
  57.0 5.2 %collective-permute-start.12 = (f32[8,8,128]{2,1,0:T(8,128)S(1)}, f32[8,8,128]{2,1,0:T(8,128)S(1)}, u32[]{:S(2)}, u32[]{:S(2)}) collective-permute-start(f32[8,8,128]{2,1,0:T(8,128)S(1)} %get-tuple-element.72.refs_0_), channel_id=1, source_target_pairs={{0,16},{8,24},{16,0},{24,8},{1,17},{9,25},{17,1},{25,9},{2,18},{10... | collective-permute-start | bytes 98312 | tf_op jit(solution)/shard_map/ppermute | solution.py:290
  59.7 5.1 %collective-permute-start.13 = (f32[8,8,128]{2,1,0:T(8,128)S(1)}, f32[8,8,128]{2,1,0:T(8,128)S(1)}, u32[]{:S(2)}, u32[]{:S(2)}) collective-permute-start(f32[8,8,128]{2,1,0:T(8,128)S(1)} %get-tuple-element.75.refs_0_), channel_id=1, source_target_pairs={{0,16},{8,24},{16,0},{24,8},{1,17},{9,25},{17,1},{25,9},{2,18},{10... | collective-permute-start | bytes 98312 | tf_op jit(solution)/shard_map/ppermute | solution.py:290
  62.5 4.9 %collective-permute-start.14 = (f32[8,8,128]{2,1,0:T(8,128)S(1)}, f32[8,8,128]{2,1,0:T(8,128)S(1)}, u32[]{:S(2)}, u32[]{:S(2)}) collective-permute-start(f32[8,8,128]{2,1,0:T(8,128)S(1)} %get-tuple-element.80.refs_2_), channel_id=1, source_target_pairs={{0,16},{8,24},{16,0},{24,8},{1,17},{9,25},{17,1},{25,9},{2,18},{10... | collective-permute-start | bytes 98312 | tf_op jit(solution)/shard_map/ppermute | solution.py:290
  67.4 6.7 %collective-permute-start.16 = (f32[16,8,128]{2,1,0:T(8,128)S(1)}, f32[16,8,128]{2,1,0:T(8,128)S(1)}, u32[]{:S(2)}, u32[]{:S(2)}) collective-permute-start(f32[16,8,128]{2,1,0:T(8,128)S(1)} %join.8.refs_0_.refs_2_), channel_id=1, source_target_pairs={{0,8},{8,0},{16,24},{24,16},{1,9},{9,1},{17,25},{25,17},{2,10},{10... | collective-permute-start | bytes 196616 | tf_op jit(solution)/shard_map/ppermute | solution.py:290
  68.9 5.2 %collective-permute-start.15 = (f32[8,8,128]{2,1,0:T(8,128)S(1)}, f32[8,8,128]{2,1,0:T(8,128)S(1)}, u32[]{:S(2)}, u32[]{:S(2)}) collective-permute-start(f32[8,8,128]{2,1,0:T(8,128)S(1)} %get-tuple-element.81.refs_2_), channel_id=1, source_target_pairs={{0,16},{8,24},{16,0},{24,8},{1,17},{9,25},{17,1},{25,9},{2,18},{10... | collective-permute-start | bytes 98312 | tf_op jit(solution)/shard_map/ppermute | solution.py:290
  74.1 5.5 %collective-permute-start.18 = (f32[32,8,128]{2,1,0:T(8,128)S(1)}, f32[32,8,128]{2,1,0:T(8,128)S(1)}, u32[]{:S(2)}, u32[]{:S(2)}) collective-permute-start(f32[32,8,128]{2,1,0:T(8,128)S(1)} %join.10.refs_0_.refs_2_), channel_id=1, source_target_pairs={{0,4},{1,5},{2,6},{3,7},{4,0},{5,1},{6,2},{7,3},{8,12},{9,13},{10,... | collective-permute-start | bytes 393224 | tf_op jit(solution)/shard_map/ppermute | solution.py:290
  75.4 4.3 %collective-permute-start.17 = (f32[16,8,128]{2,1,0:T(8,128)S(1)}, f32[16,8,128]{2,1,0:T(8,128)S(1)}, u32[]{:S(2)}, u32[]{:S(2)}) collective-permute-start(f32[16,8,128]{2,1,0:T(8,128)S(1)} %join.9.refs_0_.refs_2_), channel_id=1, source_target_pairs={{0,8},{8,0},{16,24},{24,16},{1,9},{9,1},{17,25},{25,17},{2,10},{10... | collective-permute-start | bytes 196616 | tf_op jit(solution)/shard_map/ppermute | solution.py:290
  79.7 7.9 %collective-permute-start.20 = (f32[64,8,128]{2,1,0:T(8,128)S(1)}, f32[64,8,128]{2,1,0:T(8,128)S(1)}, u32[]{:S(2)}, u32[]{:S(2)}) collective-permute-start(f32[64,8,128]{2,1,0:T(8,128)S(1)} %join.12.refs_0_.refs_2_), channel_id=1, source_target_pairs={{0,2},{1,3},{2,0},{3,1},{4,6},{5,7},{6,4},{7,5},{8,10},{9,11},{10,... | collective-permute-start | bytes 786440 | tf_op jit(solution)/shard_map/ppermute | solution.py:290
  81.2 6.3 %collective-permute-start.19 = (f32[32,8,128]{2,1,0:T(8,128)S(1)}, f32[32,8,128]{2,1,0:T(8,128)S(1)}, u32[]{:S(2)}, u32[]{:S(2)}) collective-permute-start(f32[32,8,128]{2,1,0:T(8,128)S(1)} %join.11.refs_0_.refs_2_), channel_id=1, source_target_pairs={{0,2},{1,3},{2,0},{3,1},{4,6},{5,7},{6,4},{7,5},{8,10},{9,11},{10,... | collective-permute-start | bytes 393224 | tf_op jit(solution)/shard_map/ppermute | solution.py:290
  87.6 6.3 %collective-permute-start.21 = (f32[128,8,128]{2,1,0:T(8,128)S(1)}, f32[128,8,128]{2,1,0:T(8,128)S(1)}, u32[]{:S(2)}, u32[]{:S(2)}) collective-permute-start(f32[128,8,128]{2,1,0:T(8,128)S(1)} %join.14.refs_0_.refs_5_), channel_id=1, source_target_pairs={{0,1},{1,0},{2,3},{3,2},{4,5},{5,4},{6,7},{7,6},{8,9},{9,8},{10,11... | collective-permute-start | bytes 1572872 | tf_op jit(solution)/shard_map/ppermute | solution.py:290
  87.7 11.5 %collective-permute-start.22 = (f32[64,8,128]{2,1,0:T(8,128)S(1)}, f32[64,8,128]{2,1,0:T(8,128)S(1)}, u32[]{:S(2)}, u32[]{:S(2)}) collective-permute-start(f32[64,8,128]{2,1,0:T(8,128)S(1)} %join.13.refs_0_.refs_2_), channel_id=1, source_target_pairs={{0,4},{1,5},{2,6},{3,7},{4,0},{5,1},{6,2},{7,3},{8,12},{9,13},{10,... | collective-permute-start | bytes 786440 | tf_op jit(solution)/shard_map/ppermute | solution.py:290
  99.3 5.5 %collective-permute-start.23 = (f32[128,8,128]{2,1,0:T(8,128)S(1)}, f32[128,8,128]{2,1,0:T(8,128)S(1)}, u32[]{:S(2)}, u32[]{:S(2)}) collective-permute-start(f32[128,8,128]{2,1,0:T(8,128)S(1)} %join.15.refs_0_.refs_5_), channel_id=1, source_target_pairs={{0,1},{1,0},{2,3},{3,2},{4,5},{5,4},{6,7},{7,6},{8,9},{9,8},{10,11... | collective-permute-start | bytes 1572872 | tf_op jit(solution)/shard_map/ppermute | solution.py:290
